TPU v7x, 32 devices: a whole 2x2x4 slice. The times are simulated.
32 devices in a mesh: head: 4 (over y, x), seq: 8 (over z, core).
Axes of the slice: x: 2, y: 2, z: 4, core: 2. Of those that a mesh axis runs over, the one named last changes fastest.
Arguments:
- tile_features: bfloat16 [8, 4, 512, 768], P('seq', 'head'), may hold values from -6 to 6
- slide_lengths: int32 [2], replicated, may hold values from 1025 to 10240, as said below
- qkv_weight: bfloat16 [768, 3, 768], P(None, None, 'head'), may hold values from -0.21875 to 0.21875
- qv_bias: float32 [2, 768], P(None, 'head'), may hold values from -2 to 2
- out_weight: bfloat16 [768, 768], P('head'), may hold values from -6 to 6
- out_bias: float32 [768], replicated, may hold values from -3 to 3
- attn_gain: float32 [768], replicated, may hold values from 0.5 to 1.5
- attn_shift: float32 [768], replicated, may hold values from -0.08 to 0.08
- mlp_gain: float32 [768], replicated, may hold values from 0.5 to 1.5
- mlp_shift: float32 [768], replicated, may hold values from -2 to 2
- up_weight: bfloat16 [768, 3072], P(None, 'head'), may hold values from -0.21875 to 0.21875
- up_bias: float32 [3072], P('head'), may hold values from -3 to 3
- down_weight: bfloat16 [3072, 768], P('head'), may hold values from -0.109375 to 0.109375
- down_bias: float32 [768], replicated, may hold values from -3 to 3
- output_cotangent: bfloat16 [8, 4, 512, 768], P('seq', 'head'), may hold values from -6 to 6
Outputs:
- output: bfloat16 [8, 4, 512, 768], P('seq', 'head')
- grad_features: float32 [8, 4, 512, 768], P('seq', 'head')
- grad_qkv_weight: float32 [768, 3, 768], P(None, None, 'head')
- grad_qv_bias: float32 [2, 768], P(None, 'head')
- grad_out_weight: float32 [768, 768], P('head')
- grad_out_bias: float32 [768], replicated
- grad_attn_gain: float32 [768], replicated
- grad_attn_shift: float32 [768], replicated
- grad_mlp_gain: float32 [768], replicated
- grad_mlp_shift: float32 [768], replicated
- grad_up_weight: float32 [768, 3072], P(None, 'head')
- grad_up_bias: float32 [3072], P('head')
- grad_down_weight: float32 [3072, 768], P('head')
- grad_down_bias: float32 [768], replicated
Inputs may be any that keep to these rules, and one draw needn't show every extreme that they name: Slide k holds slide_lengths[k] valid tiles followed by padding up to a whole number of 1024-tile blocks, two or more; the slides lie one after another from tile 0 and fill all 16384 tiles exactly.
All inputs are finite; a program needn't handle non-finite values.
Results may differ from a plain program's by a relative error of at most 0.02.
Values may be sent and summed in bfloat16 or wider, within the bound.
A program may use at most 256 MiB of HBM per device.

v0:
```python
import jax
import jax.numpy as jnp
from jax import lax
from jax.sharding import PartitionSpec as P

HEAD_WIDTH = 48
SEGMENT_TILES = 1024


epsilon = 1e-05
masked_low = -1e30


def from_partner(x, axis, stride):
    return lax.ppermute(x, axis, [(i, i ^ 1 << stride) for i in range(lax.axis_size(axis))])


def layout(slide_lengths, positions):
    blocks = (slide_lengths + SEGMENT_TILES - 1) // SEGMENT_TILES
    slide_ends = jnp.cumsum(blocks) * SEGMENT_TILES
    slide_starts = slide_ends - blocks * SEGMENT_TILES
    inside = (positions[..., None] >= slide_starts) & (positions[..., None] < slide_ends)
    labels = jnp.arange(slide_lengths.shape[0], dtype=jnp.int32)
    slide_index = jnp.sum(jnp.where(inside, labels, 0), axis=-1)
    offset = positions - jnp.sum(jnp.where(inside, slide_starts, 0), axis=-1)
    length = jnp.sum(jnp.where(inside, slide_lengths, 0), axis=-1)
    return (slide_index, offset < length)


def matmul(left_side, right_side):
    return jnp.dot(left_side, right_side, preferred_element_type=jnp.float32)


def inner_last(left_side, right_side):
    return lax.dot_general(
        left_side, right_side, (((1,), (1,)), ((), ())), preferred_element_type=jnp.float32
    )


def inner_first(left_side, right_side):
    return lax.dot_general(
        left_side, right_side, (((0,), (0,)), ((), ())), preferred_element_type=jnp.float32
    )


def norm_forward(values, norm_gain, norm_shift):
    center = values - jnp.mean(values, axis=-1, keepdims=True)
    inverse = lax.rsqrt(jnp.mean(center * center, axis=-1, keepdims=True) + epsilon)
    normed = center * inverse
    return (normed * norm_gain + norm_shift, normed, inverse)


def norm_backward(grad_out, normed, inverse, norm_gain):
    scaled = grad_out * norm_gain
    return inverse * (
        scaled
        - jnp.mean(scaled, axis=-1, keepdims=True)
        - normed * jnp.mean(scaled * normed, axis=-1, keepdims=True)
    )


def gelu_tanh(values):
    return jax.nn.gelu(values, approximate=True)


def dilate(source, dilation_step, phase):
    folded = source.reshape((source.shape[0] // dilation_step, dilation_step) + source.shape[1:])
    return lax.dynamic_index_in_dim(folded, phase, axis=1, keepdims=False)


def undilate(values, dilation_step, phase, fill_value):
    marks = jnp.arange(dilation_step, dtype=jnp.int32) == phase
    marks = marks.reshape((1, dilation_step) + (1,) * (values.ndim - 1))
    folded = jnp.where(marks, values[:, None], jnp.asarray(fill_value, values.dtype))
    return folded.reshape((values.shape[0] * dilation_step,) + values.shape[1:])


def attend(query_rows, query_slide, key_rows, value_rows, key_slide, key_valid, score_scale):
    allowed = (query_slide[:, None] == key_slide[None, :]) & key_valid[None, :]
    scores = inner_last(query_rows, key_rows) * score_scale
    masked = jnp.where(allowed, scores, masked_low)
    row_maximum = jnp.max(masked, axis=1)
    weights = jnp.where(allowed, jnp.exp(masked - row_maximum[:, None]), 0.0)
    return (row_maximum, jnp.sum(weights, axis=1), matmul(weights.astype(jnp.bfloat16), value_rows))


def attend_back(
    query_rows,
    query_slide,
    grad_out,
    row_lse,
    row_delta,
    key_rows,
    value_rows,
    key_slide,
    key_valid,
    score_scale,
):
    allowed = (query_slide[:, None] == key_slide[None, :]) & key_valid[None, :]
    scores = inner_last(query_rows, key_rows) * score_scale
    probability = jnp.where(allowed, jnp.exp(scores - row_lse[:, None]), 0.0)
    grad_prob = inner_last(grad_out, value_rows)
    grad_score = (probability * (grad_prob - row_delta[:, None])).astype(jnp.bfloat16)
    grad_query = matmul(grad_score, key_rows) * score_scale
    grad_keys = inner_first(grad_score, query_rows) * score_scale
    grad_values = inner_first(probability.astype(jnp.bfloat16), grad_out)
    return (grad_query, grad_keys, grad_values)


def gather_over_group(source, level_bit_count, member):
    collected = source
    for bit_index in range(level_bit_count):
        partner_part = from_partner(collected, "seq", bit_index)
        bit_high = member >> bit_index & 1 == 1
        collected = jnp.where(
            bit_high,
            jnp.concatenate([partner_part, collected], axis=2),
            jnp.concatenate([collected, partner_part], axis=2),
        )
    return collected


def group_reduce(source, level_bit_count, member):
    collected = source
    for bit_index in reversed(range(level_bit_count)):
        half_size = collected.shape[2] // 2
        lower_half = collected[:, :, :half_size]
        upper_half = collected[:, :, half_size:]
        bit_high = member >> bit_index & 1 == 1
        kept_half = jnp.where(bit_high, upper_half, lower_half)
        sent_half = jnp.where(bit_high, lower_half, upper_half)
        collected = kept_half + from_partner(
            sent_half.astype(jnp.bfloat16), "seq", bit_index
        ).astype(sent_half.dtype)
    return collected


def per_device(
    tile_features,
    slide_lengths,
    qkv_weight,
    qv_bias,
    out_weight,
    out_bias,
    attn_gain,
    attn_shift,
    mlp_gain,
    mlp_shift,
    up_weight,
    up_bias,
    down_weight,
    down_bias,
    output_cotangent,
):
    row_count = tile_features.shape[2]
    model_width = tile_features.shape[3]
    local_width = qkv_weight.shape[2]
    heads_on_member = local_width // HEAD_WIDTH
    hidden_local = up_weight.shape[1]
    sequence_member = lax.axis_index("seq")
    head_rank = lax.axis_index("head")
    head_count = lax.axis_size("head")
    sequence_extent = row_count * head_count
    score_scale = HEAD_WIDTH ** (-0.5)
    features = tile_features.reshape(row_count, model_width).astype(jnp.float32)
    normed_one, hat_one, inv_one = norm_forward(features, attn_gain, attn_shift)
    normed_one = normed_one.astype(jnp.bfloat16)
    gathered_one = lax.all_gather(normed_one, "head", axis=0, tiled=True)
    qkv_flat = qkv_weight.reshape(model_width, 3 * local_width)
    bias_flat = jnp.concatenate([qv_bias[0], jnp.zeros((local_width,), jnp.float32), qv_bias[1]])
    projected = (matmul(gathered_one, qkv_flat) + bias_flat).astype(jnp.bfloat16)
    projected = projected.reshape(sequence_extent, 3, heads_on_member, HEAD_WIDTH)
    positions = sequence_member * sequence_extent + jnp.arange(sequence_extent, dtype=jnp.int32)
    slide_here, valid_here = layout(slide_lengths, positions)
    plans = []
    peak_list, total_list, numer_list = ([], [], [])
    for level_index in range(5):
        dilation_step = 2**level_index
        window = SEGMENT_TILES * dilation_step
        dilated_length = sequence_extent // dilation_step
        step_phases = [
            (head_rank * heads_on_member + head_slot) % dilation_step
            for head_slot in range(heads_on_member)
        ]
        dilated_query = jnp.stack(
            [
                dilate(projected[:, 0, head_slot], dilation_step, step_phases[head_slot])
                for head_slot in range(heads_on_member)
            ]
        )
        dilated_keys = jnp.stack(
            [
                dilate(projected[:, 1, head_slot], dilation_step, step_phases[head_slot])
                for head_slot in range(heads_on_member)
            ]
        )
        dilated_values = jnp.stack(
            [
                dilate(projected[:, 2, head_slot], dilation_step, step_phases[head_slot])
                for head_slot in range(heads_on_member)
            ]
        )
        dilated_slide = jnp.stack(
            [
                dilate(slide_here, dilation_step, step_phases[head_slot])
                for head_slot in range(heads_on_member)
            ]
        )
        dilated_valid = jnp.stack(
            [
                dilate(valid_here, dilation_step, step_phases[head_slot])
                for head_slot in range(heads_on_member)
            ]
        )
        if window <= sequence_extent:
            slide_block_count = heads_on_member * (dilated_length // SEGMENT_TILES)
            block_row_count = SEGMENT_TILES
            level_bit_count = 0
            key_details = (
                dilated_keys.reshape(slide_block_count, block_row_count, HEAD_WIDTH),
                dilated_values.reshape(slide_block_count, block_row_count, HEAD_WIDTH),
                dilated_slide.reshape(slide_block_count, block_row_count),
                dilated_valid.reshape(slide_block_count, block_row_count),
            )
        else:
            slide_block_count = heads_on_member
            block_row_count = dilated_length
            group_size = window // sequence_extent
            level_bit_count = group_size.bit_length() - 1
            gathered_key_value = gather_over_group(
                jnp.stack([dilated_keys, dilated_values]), level_bit_count, sequence_member
            )
            group_first = sequence_member // group_size * group_size * sequence_extent
            key_marks = [
                layout(
                    slide_lengths,
                    group_first
                    + step_phases[head_slot]
                    + dilation_step * jnp.arange(SEGMENT_TILES, dtype=jnp.int32),
                )
                for head_slot in range(heads_on_member)
            ]
            key_details = (
                gathered_key_value[0],
                gathered_key_value[1],
                jnp.stack([mark[0] for mark in key_marks]),
                jnp.stack([mark[1] for mark in key_marks]),
            )
        query_details = (
            dilated_query.reshape(slide_block_count, block_row_count, HEAD_WIDTH),
            dilated_slide.reshape(slide_block_count, block_row_count),
        )
        row_maximum, row_denominator, row_numerator = lax.map(
            lambda block_args: attend(*block_args, score_scale), query_details + key_details
        )
        row_maximum = row_maximum.reshape(heads_on_member, dilated_length)
        row_denominator = row_denominator.reshape(heads_on_member, dilated_length)
        row_numerator = row_numerator.reshape(heads_on_member, dilated_length, HEAD_WIDTH)
        peak_list.append(
            jnp.stack(
                [
                    undilate(
                        row_maximum[head_slot], dilation_step, step_phases[head_slot], masked_low
                    )
                    for head_slot in range(heads_on_member)
                ]
            )
        )
        total_list.append(
            jnp.stack(
                [
                    undilate(row_denominator[head_slot], dilation_step, step_phases[head_slot], 0.0)
                    for head_slot in range(heads_on_member)
                ]
            )
        )
        numer_list.append(
            jnp.stack(
                [
                    undilate(row_numerator[head_slot], dilation_step, step_phases[head_slot], 0.0)
                    for head_slot in range(heads_on_member)
                ]
            )
        )
        plans.append(
            (
                dilation_step,
                step_phases,
                slide_block_count,
                block_row_count,
                level_bit_count,
                dilated_length,
                query_details,
                key_details,
            )
        )
    peaks = jnp.stack(peak_list)
    best_peak = jnp.max(peaks, axis=0)
    factor = jnp.exp(peaks - best_peak)
    denom_all = jnp.sum(factor * jnp.stack(total_list), axis=0)
    attention = jnp.sum(factor[..., None] * jnp.stack(numer_list), axis=0) / denom_all[..., None]
    log_total = best_peak + jnp.log(denom_all)
    attn_rounded = (
        attention.transpose(1, 0, 2).reshape(sequence_extent, local_width).astype(jnp.bfloat16)
    )
    attn_rows = lax.psum_scatter(
        matmul(attn_rounded, out_weight).astype(jnp.bfloat16),
        "head",
        scatter_dimension=0,
        tiled=True,
    ).astype(jnp.float32)
    residual = features + attn_rows + out_bias
    normed_two, hat_two, inv_two = norm_forward(residual, mlp_gain, mlp_shift)
    normed_two = normed_two.astype(jnp.bfloat16)
    gathered_two = lax.all_gather(normed_two, "head", axis=0, tiled=True)
    pre_act = matmul(gathered_two, up_weight) + up_bias
    hidden = gelu_tanh(pre_act).astype(jnp.bfloat16)
    mlp_rows = lax.psum_scatter(
        matmul(hidden, down_weight).astype(jnp.bfloat16), "head", scatter_dimension=0, tiled=True
    ).astype(jnp.float32)
    result = residual + mlp_rows + down_bias
    output = result.astype(jnp.bfloat16).reshape(tile_features.shape)
    grad_result = output_cotangent.reshape(row_count, model_width)
    grad_res32 = grad_result.astype(jnp.float32)
    shard_rows = lax.all_gather(grad_result, "head", axis=0, tiled=True)
    joined_down = jnp.concatenate(
        [inner_last(shard_rows, down_weight), shard_rows.astype(jnp.float32)], axis=1
    )
    grad_hidden = joined_down[:, :hidden_local]
    grad_down = inner_first(hidden, joined_down[:, hidden_local:].astype(jnp.bfloat16))
    grad_gelu = jax.vjp(gelu_tanh, pre_act)[1](grad_hidden)[0]
    grad_pre = grad_gelu.astype(jnp.bfloat16)
    grad_up_bias = jnp.sum(grad_pre.astype(jnp.float32), axis=0)
    grad_up = inner_first(lax.all_gather(normed_two, "head", axis=0, tiled=True), grad_pre)
    grad_normed_two = lax.psum_scatter(
        inner_last(grad_pre, up_weight).astype(jnp.bfloat16),
        "head",
        scatter_dimension=0,
        tiled=True,
    ).astype(jnp.float32)
    grad_mlp_gain = jnp.sum(grad_normed_two * hat_two, axis=0)
    grad_mlp_shift = jnp.sum(grad_normed_two, axis=0)
    grad_residual = grad_res32 + norm_backward(grad_normed_two, hat_two, inv_two, mlp_gain)
    grad_down_bias = jnp.sum(grad_res32, axis=0)
    grad_out_bias = jnp.sum(grad_residual, axis=0)
    grad_res_low = grad_residual.astype(jnp.bfloat16)
    shard_rows = lax.all_gather(grad_res_low, "head", axis=0, tiled=True)
    joined_out = jnp.concatenate(
        [inner_last(shard_rows, out_weight), shard_rows.astype(jnp.float32)], axis=1
    )
    grad_attn_full = joined_out[:, :local_width]
    grad_out = inner_first(attn_rounded, joined_out[:, local_width:].astype(jnp.bfloat16))
    grad_attn = (
        grad_attn_full.astype(jnp.bfloat16)
        .reshape(sequence_extent, heads_on_member, HEAD_WIDTH)
        .transpose(1, 0, 2)
    )
    delta_all = jnp.sum(grad_attn.astype(jnp.float32) * attention, axis=-1)
    grad_queries = jnp.zeros((heads_on_member, sequence_extent, HEAD_WIDTH), jnp.float32)
    grad_keys = jnp.zeros((heads_on_member, sequence_extent, HEAD_WIDTH), jnp.float32)
    grad_values = jnp.zeros((heads_on_member, sequence_extent, HEAD_WIDTH), jnp.float32)
    for dilation_layout in plans:
        (
            dilation_step,
            step_phases,
            slide_block_count,
            block_row_count,
            level_bit_count,
            dilated_length,
            query_details,
            key_details,
        ) = dilation_layout
        dilated_gradient = jnp.stack(
            [
                dilate(grad_attn[head_slot], dilation_step, step_phases[head_slot])
                for head_slot in range(heads_on_member)
            ]
        )
        dilated_log_sum_exp = jnp.stack(
            [
                dilate(log_total[head_slot], dilation_step, step_phases[head_slot])
                for head_slot in range(heads_on_member)
            ]
        )
        dilated_delta = jnp.stack(
            [
                dilate(delta_all[head_slot], dilation_step, step_phases[head_slot])
                for head_slot in range(heads_on_member)
            ]
        )
        back_args = (
            query_details[0],
            query_details[1],
            dilated_gradient.reshape(slide_block_count, block_row_count, HEAD_WIDTH),
            dilated_log_sum_exp.reshape(slide_block_count, block_row_count),
            dilated_delta.reshape(slide_block_count, block_row_count),
        ) + key_details
        query_per_level, keys_per_level, values_per_level = lax.map(
            lambda block_args: attend_back(*block_args, score_scale), back_args
        )
        query_per_level = query_per_level.reshape(heads_on_member, dilated_length, HEAD_WIDTH)
        if level_bit_count == 0:
            keys_per_level = keys_per_level.reshape(heads_on_member, dilated_length, HEAD_WIDTH)
            values_per_level = values_per_level.reshape(heads_on_member, dilated_length, HEAD_WIDTH)
        else:
            returned = group_reduce(
                jnp.stack([keys_per_level, values_per_level]), level_bit_count, sequence_member
            )
            keys_per_level = returned[0]
            values_per_level = returned[1]
        grad_queries = grad_queries + jnp.stack(
            [
                undilate(query_per_level[head_slot], dilation_step, step_phases[head_slot], 0.0)
                for head_slot in range(heads_on_member)
            ]
        )
        grad_keys = grad_keys + jnp.stack(
            [
                undilate(keys_per_level[head_slot], dilation_step, step_phases[head_slot], 0.0)
                for head_slot in range(heads_on_member)
            ]
        )
        grad_values = grad_values + jnp.stack(
            [
                undilate(values_per_level[head_slot], dilation_step, step_phases[head_slot], 0.0)
                for head_slot in range(heads_on_member)
            ]
        )
    grad_proj = (
        jnp.stack([grad_queries, grad_keys, grad_values])
        .transpose(2, 0, 1, 3)
        .reshape(sequence_extent, 3 * local_width)
        .astype(jnp.bfloat16)
    )
    part_sums = jnp.sum(
        grad_proj.astype(jnp.float32).reshape(sequence_extent, 3, local_width), axis=0
    )
    grad_qv = jnp.stack([part_sums[0], part_sums[2]])
    grad_qkv = inner_first(lax.all_gather(normed_one, "head", axis=0, tiled=True), grad_proj)
    grad_qkv = grad_qkv.reshape(model_width, 3, local_width)
    grad_normed_one = lax.psum_scatter(
        inner_last(grad_proj, qkv_flat).astype(jnp.bfloat16),
        "head",
        scatter_dimension=0,
        tiled=True,
    ).astype(jnp.float32)
    grad_attn_gain = jnp.sum(grad_normed_one * hat_one, axis=0)
    grad_attn_shift = jnp.sum(grad_normed_one, axis=0)
    grad_features = grad_residual + norm_backward(grad_normed_one, hat_one, inv_one, attn_gain)
    summed = (
        lax.psum(grad_qkv.astype(jnp.bfloat16), "seq").astype(jnp.float32),
        lax.psum(grad_qv.astype(jnp.bfloat16), "seq").astype(jnp.float32),
        lax.psum(grad_out.astype(jnp.bfloat16), "seq").astype(jnp.float32),
        lax.psum(grad_up.astype(jnp.bfloat16), "seq").astype(jnp.float32),
        lax.psum(grad_up_bias.astype(jnp.bfloat16), "seq").astype(jnp.float32),
        lax.psum(grad_down.astype(jnp.bfloat16), "seq").astype(jnp.float32),
    )
    norm_totals = lax.psum(
        (
            grad_attn_gain,
            grad_attn_shift,
            grad_mlp_gain,
            grad_mlp_shift,
            grad_out_bias,
            grad_down_bias,
        ),
        ("head", "seq"),
    )
    return (
        output,
        grad_features.reshape(tile_features.shape),
        summed[0],
        summed[1],
        summed[2],
        norm_totals[4],
        norm_totals[0],
        norm_totals[1],
        norm_totals[2],
        norm_totals[3],
        summed[3],
        summed[4],
        summed[5],
        norm_totals[5],
    )


def solution(mesh):
    in_specs = (
        P("seq", "head", None, None),
        P(),
        P(None, None, "head"),
        P(None, "head"),
        P("head", None),
        P(),
        P(),
        P(),
        P(),
        P(),
        P(None, "head"),
        P("head"),
        P("head", None),
        P(),
        P("seq", "head", None, None),
    )
    out_specs = (
        P("seq", "head", None, None),
        P("seq", "head", None, None),
        P(None, None, "head"),
        P(None, "head"),
        P("head", None),
        P(),
        P(),
        P(),
        P(),
        P(),
        P(None, "head"),
        P("head"),
        P("head", None),
        P(),
    )
    return jax.shard_map(
        per_device, mesh=mesh, in_specs=in_specs, out_specs=out_specs, check_vma=False
    )
```

profile of v0, /device:TPU:0, one launch (start us, length us, event | category | flops | bytes accessed | tf_op | source)
XLA Modules:
  0.0 1516.0 jit_solution(9677259973413603258)
XLA Ops:
  37.8 21.9 %all-gather.6.cloned.1.call-done = bf16[2048,768]{1,0:T(8,128)(2,1)} async-done(((bf16[512,768]{1,0:T(8,128)(2,1)}), bf16[2048,768]{1,0:T(8,128)(2,1)}) %all-gather.6.cloned.1.call-update) | async-done | bytes 3145744 | tf_op jit(solution)/shard_map/all_gather | solution.py:168
  78.1 112.9 %while.142 = (s32[]{:T(128)}, f32[8,1024]{1,0:T(8,128)S(1)}, f32[8,1024]{1,0:T(8,128)}, f32[8,1024,48]{1,2,0:T(8,128)}, s32[8,1024]{1,0:T(8,128)}, /*index=5*/pr...) while((s32[]{:T(128)}, f32[8,1024]{1,0:T(8,128)S(1)}, ...), condition=%wide.region_9.10_spmd, body=%wide.region_6.9_spmd.sunk | while | flops 221247488 | bytes 13634693 | solution.py:253
  251.7 48.3 %while.143 = (s32[]{:T(128)}, f32[4,1024]{1,0:T(4,128)S(1)}, f32[4,1024]{1,0:T(4,128)}, f32[4,1024,48]{1,2,0:T(8,128)}, s32[4,1024]{1,0:T(4,128)S(1)}, /*index=5...) while((s32[]{:T(128)}, f32[4,1024]{1,0:T(4,128)S(1)}, ...), condition=%wide.region_13.14_spmd, body=%wide.region_10.13_spmd.sunk | while | flops 221247488 | bytes 13634693 | solution.py:253
  440.3 25.9 %while.144 = (s32[]{:T(128)}, f32[4,512]{1,0:T(4,128)S(1)}, f32[4,512]{1,0:T(4,128)S(1)}, f32[4,512,48]{1,2,0:T(8,128)}, s32[4,512]{1,0:T(4,128)}, /*index=5*/s3...) while((s32[]{:T(128)}, f32[4,512]{1,0:T(4,128)S(1)}, ...), condition=%wide.region_29.30_spmd, body=%wide.region_26.29_spmd.sunk | while | flops 108526592 | bytes 7099537 | solution.py:253
  485.5 16.3 %while.145 = (s32[]{:T(128)}, f32[4,256]{1,0:T(4,128)S(1)}, f32[4,256]{1,0:T(4,128)S(1)}, f32[4,256,48]{1,2,0:T(8,128)S(1)}, s32[4,256]{1,0:T(4,128)S(1)}, /*ind...) while((s32[]{:T(128)}, f32[4,256]{1,0:T(4,128)S(1)}, ...), condition=%wide.region_45.46_spmd, body=%wide.region_42.45_spmd.sunk | while | flops 54263296 | bytes 3825809 | solution.py:253
  515.8 19.3 %while.146 = (s32[]{:T(128)}, f32[4,128]{1,0:T(4,128)S(1)}, f32[4,128]{1,0:T(4,128)}, f32[4,128,48]{1,2,0:T(8,128)S(1)}, s32[4,128]{1,0:T(4,128)}, /*index=5*/s3...) while((s32[]{:T(128)}, f32[4,128]{1,0:T(4,128)S(1)}, ...), condition=%wide.region_61.62_spmd, body=%wide.region_58.61_spmd.sunk | while | flops 27131648 | bytes 2188945 | solution.py:253
  561.1 42.5 %reduce-scatter.5.cloned.1.call-done = bf16[512,768]{1,0:T(8,128)(2,1)} async-done(((bf16[2048,768]{1,0:T(8,128)(2,1)}), bf16[512,768]{1,0:T(8,128)(2,1)}) %reduce-scatter.5.cloned.1.call-update) | async-done | bytes 786448 | tf_op jit(solution)/shard_map/reduce_scatter | solution.py:306
  607.7 43.5 %all-gather.8.cloned.1.call-done = bf16[2048,768]{1,0:T(8,128)(2,1)} async-done(((bf16[512,768]{1,0:T(8,128)(2,1)}), bf16[2048,768]{1,0:T(8,128)(2,1)}) %all-gather.8.cloned.1.call-update) | async-done | bytes 3145744 | tf_op jit(solution)/shard_map/all_gather | solution.py:315
  658.6 38.3 %all-gather.12.cloned.1.call-done = bf16[1,1,2048,768]{3,2,1,0:T(8,128)(2,1)} async-done(((bf16[1,1,512,768]{3,2,1,0:T(8,128)(2,1)}), bf16[1,1,2048,768]{3,2,1,0:T(8,128)(2,1)}) %all-gather.12.cloned.1.call-update) | async-done | bytes 3145744 | tf_op jit(solution)/shard_map/all_gather | solution.py:325
  696.8 11.0 fusion.357
  713.6 8.5 convolution_convert_fusion.1
  722.3 35.4 %reduce-scatter.9.cloned.1.call-done = bf16[512,768]{1,0:T(8,128)(2,1)} async-done(((bf16[2048,768]{1,0:T(8,128)(2,1)}), bf16[512,768]{1,0:T(8,128)(2,1)}) %reduce-scatter.9.cloned.1.call-update) | async-done | bytes 786448 | tf_op jit(solution)/shard_map/reduce_scatter | solution.py:335
  760.5 44.0 %reduce-scatter.7.cloned.1.call-done = bf16[512,768]{1,0:T(8,128)(2,1)} async-done(((bf16[2048,768]{1,0:T(8,128)(2,1)}), bf16[512,768]{1,0:T(8,128)(2,1)}) %reduce-scatter.7.cloned.1.call-update) | async-done | bytes 786448 | tf_op jit(solution)/shard_map/reduce_scatter | solution.py:318
  834.8 7.6 fusion.309
  842.4 12.0 all-gather.10.cloned.1.call-done
  873.5 104.5 %while.147 = (s32[]{:T(128)}, f32[8,1024,48]{1,2,0:T(8,128)S(1)}, f32[8,1024,48]{1,2,0:T(8,128)}, f32[8,1024,48]{1,2,0:T(8,128)}, s32[8,1024]{1,0:T(8,128)}, /*i...) while((s32[]{:T(128)}, f32[8,1024,48]{1,2,0:T(8,128)S(1)}, ...), condition=%wide.region_73.74_spmd, body=%wide.region_72.73_spmd.sunk | while | flops 518094848 | bytes 21361808 | solution.py:398
  1002.4 38.6 %while.148 = (s32[]{:T(128)}, f32[4,1024,48]{1,2,0:T(8,128)}, f32[4,1024,48]{1,2,0:T(8,128)}, f32[4,1024,48]{1,2,0:T(8,128)}, s32[4,1024]{1,0:T(4,128)}, /*index...) while((s32[]{:T(128)}, f32[4,1024,48]{1,2,0:T(8,128)}, ...), condition=%wide.region_75.76_spmd, body=%wide.region_74.75_spmd.sunk | while | flops 518094848 | bytes 22607020 | solution.py:398
  1074.6 36.4 %while.149 = (s32[]{:T(128)}, f32[4,512,48]{1,2,0:T(8,128)}, f32[4,1024,48]{1,2,0:T(8,128)S(1)}, f32[4,1024,48]{1,2,0:T(8,128)S(1)}, s32[4,512]{1,0:T(4,128)}, /...) while((s32[]{:T(128)}, f32[4,512,48]{1,2,0:T(8,128)}, ...), condition=%wide.region_77.78_spmd, body=%wide.region_76.77_spmd.sunk | while | flops 256450560 | bytes 11114653 | solution.py:398
  1125.3 32.2 %while.150 = (s32[]{:T(128)}, f32[4,256,48]{1,2,0:T(8,128)}, f32[4,1024,48]{1,2,0:T(8,128)S(1)}, f32[4,1024,48]{1,2,0:T(8,128)S(1)}, s32[4,256]{1,0:T(4,128)}, /...) while((s32[]{:T(128)}, f32[4,256,48]{1,2,0:T(8,128)}, ...), condition=%wide.region_79.80_spmd, body=%wide.region_78.79_spmd.sunk | while | flops 128249856 | bytes 6157469 | solution.py:398
  1172.4 25.0 %while.151 = (s32[]{:T(128)}, f32[4,128,48]{1,2,0:T(8,128)S(1)}, f32[4,1024,48]{1,2,0:T(8,128)S(1)}, f32[4,1024,48]{1,2,0:T(8,128)S(1)}, s32[4,128]{1,0:T(4,128)...) while((s32[]{:T(128)}, f32[4,128,48]{1,2,0:T(8,128)S(1)}, ...), condition=%wide.region_81.82_spmd, body=%wide.region_80.81_spmd.sunk | while | flops 64149504 | bytes 3678877 | solution.py:398
  1338.4 16.1 %all-reduce.1 = (bf16[2,192]{1,0:T(2,128)(2,1)S(1)}, bf16[768]{0:T(1024)(128)(2,1)S(1)}) all-reduce(bf16[2,192]{1,0:T(2,128)(2,1)S(1)} %pad_maximum_fusion.33, bf16[768]{0:T(1024)(128)(2,1)S(1)} %copy-done.369), channel_id=1, replica_groups=mesh['head'=4,'seq'=8] {'seq'}, use_global_device_ids=true, to_apply=%region_87.88 | all-reduce | flops 1152 | bytes 4608 | tf_op jit(solution)/shard_map/psum | solution.py:452
  1355.6 59.3 %all-reduce.5.cloned.1.call-done = (bf16[768,3,192]{0,2,1:T(8,128)(2,1)}, bf16[192,768]{1,0:T(8,128)(2,1)}, bf16[768,768]{1,0:T(8,128)(2,1)}, bf16[768,768]{1,0:T(8,128)(2,1)}) async-done(((bf16[768,3,192]{0,2,1:T(8,128)(2,1)}, bf16[192,768]{1,0:T(8,128)(2,1)}, bf16[768,768]{1,0:T(8,128)(2,1)}, bf16[768,768]{1,0:T(8,128)(2,1)}), (bf16[768,3,192]{0,2,1:T(8,128)(2,1)}, bf16[192,768]{1,0:T(8,128)(2,1)}, ...) | async-done | bytes 3538960 | tf_op jit(solution)/shard_map/psum | solution.py:451
  1421.6 40.6 %reduce-scatter.11.cloned.1.call-done = bf16[512,768]{1,0:T(8,128)(2,1)} async-done(((bf16[2048,768]{1,0:T(8,128)(2,1)}), bf16[512,768]{1,0:T(8,128)(2,1)}) %reduce-scatter.11.cloned.1.call-update) | async-done | bytes 786448 | tf_op jit(solution)/shard_map/reduce_scatter | solution.py:441
  1465.9 40.2 %all-reduce = (f32[768]{0:T(1024)}, f32[768]{0:T(1024)}, f32[768]{0:T(1024)}, f32[768]{0:T(1024)}, f32[768]{0:T(1024)}, /*index=5*/f32[768]{0:T(1024)}) all-reduce(f32[768]{0:T(1024)} %get-tuple-element.1551, f32[768]{0:T(1024)} %get-tuple-element.1211, ...), channel_id=1, replica_groups=mesh['head'=4,'seq'=8] {'head','seq'}, use_global_device_ids=true, to_apply=%region_90.91 | all-reduce | flops 4608 | bytes 36864 | tf_op jit(solution)/shard_map/psum | solution.py:458
  (2006 shorter events, 1070.8 us)
Async XLA Ops:
  7.2 689.7 %copy-start = (bf16[768,768]{1,0:T(8,128)(2,1)S(1)}, bf16[768,768]{1,0:T(8,128)(2,1)}, u32[]{:S(2)}) copy-start(bf16[768,768]{1,0:T(8,128)(2,1)} %param.47) | copy-start | bytes 3538948
  7.2 52.4 %all-gather.6.cloned.1.call-start = ((), (), s32[]{:S(2)}) async-start(), calls=%async_computation.4 | async-start | bytes 3932160 | tf_op jit(solution)/shard_map/all_gather | solution.py:168
  12.8 590.8 %reduce-scatter.5.cloned.1.call-start = ((), (), s32[]{:S(2)}) async-start(), calls=%async_computation.5 | async-start | bytes 3932160 | tf_op jit(solution)/shard_map/reduce_scatter | solution.py:306
  348.4 87.0 %collective-permute-start = (bf16[2,4,512,48]{2,3,1,0:T(8,128)(2,1)}, bf16[2,4,512,48]{2,3,1,0:T(8,128)(2,1)}, u32[]{:S(2)}, u32[]{:S(2)}) collective-permute-start(bf16[2,4,512,48]{2,3,1,0:T(8,128)(2,1)} %pad_maximum_fusion.9), channel_id=1, source_target_pairs={{0,1},{1,0},{2,3},{3,2},{4,5},{5,4},{6,7},{7,6},{8,9},{9,8},{10,11... | collective-permute-start | bytes 1179656 | tf_op jit(solution)/shard_map/ppermute | solution.py:15
  384.3 42.6 %collective-permute-start.1 = (bf16[2,4,256,48]{2,3,1,0:T(8,128)(2,1)}, bf16[2,4,256,48]{2,3,1,0:T(8,128)(2,1)}, u32[]{:S(2)}, u32[]{:S(2)}) collective-permute-start(bf16[2,4,256,48]{2,3,1,0:T(8,128)(2,1)} %pad_maximum_fusion.12), channel_id=1, source_target_pairs={{0,1},{1,0},{2,3},{3,2},{4,5},{5,4},{6,7},{7,6},{8,9},{9,8},{10,11... | collective-permute-start | bytes 589832 | tf_op jit(solution)/shard_map/ppermute | solution.py:15
  395.6 28.0 %collective-permute-start.3 = (bf16[2,4,128,48]{2,3,1,0:T(8,128)(2,1)}, bf16[2,4,128,48]{2,3,1,0:T(8,128)(2,1)}, u32[]{:S(2)}, u32[]{:S(2)}) collective-permute-start(bf16[2,4,128,48]{2,3,1,0:T(8,128)(2,1)} %pad_maximum_fusion.15), channel_id=1, source_target_pairs={{0,1},{1,0},{2,3},{3,2},{4,5},{5,4},{6,7},{7,6},{8,9},{9,8},{10,11... | collective-permute-start | bytes 294920 | tf_op jit(solution)/shard_map/ppermute | solution.py:15
  424.6 7.4 collective-permute-start.4
  428.8 53.0 %collective-permute-start.2 = (bf16[2,4,512,48]{2,3,1,0:T(8,128)(2,1)}, bf16[2,4,512,48]{2,3,1,0:T(8,128)(2,1)}, u32[]{:S(2)}, u32[]{:S(2)}) collective-permute-start(bf16[2,4,512,48]{2,3,1,0:T(8,128)(2,1)} %maximum_select_fusion.3), channel_id=1, source_target_pairs={{0,2},{1,3},{2,0},{3,1},{4,6},{5,7},{6,4},{7,5},{8,10},{9,11},{10,... | collective-permute-start | bytes 1179656 | tf_op jit(solution)/shard_map/ppermute | solution.py:15
  432.9 79.1 %collective-permute-start.5 = (bf16[2,4,512,48]{2,3,1,0:T(8,128)(2,1)}, bf16[2,4,512,48]{2,3,1,0:T(8,128)(2,1)}, u32[]{:S(2)}, u32[]{:S(2)}) collective-permute-start(bf16[2,4,512,48]{2,3,1,0:T(8,128)(2,1)} %maximum_select_fusion.4), channel_id=1, source_target_pairs={{0,4},{1,5},{2,6},{3,7},{4,0},{5,1},{6,2},{7,3},{8,12},{9,13},{10,... | collective-permute-start | bytes 1179656 | tf_op jit(solution)/shard_map/ppermute | solution.py:15
  561.0 90.1 %all-gather.8.cloned.1.call-start = ((), (), s32[]{:S(2)}) async-start(), calls=%async_computation.6 | async-start | bytes 3932160 | tf_op jit(solution)/shard_map/all_gather | solution.py:315
  607.0 89.8 %all-gather.12.cloned.1.call-start = ((), (), s32[]{:S(2)}) async-start(), calls=%async_computation.11 | async-start | bytes 3932160 | tf_op jit(solution)/shard_map/all_gather | solution.py:325
  607.6 89.2 %copy-start.380 = (f32[768]{0:T(1024)S(1)}, f32[768]{0:T(1024)}, u32[]{:S(2)}) copy-start(f32[768]{0:T(1024)} %param.46) | copy-start | bytes 9220
  607.6 150.1 %reduce-scatter.9.cloned.1.call-start = ((), (), s32[]{:S(2)}) async-start(), calls=%async_computation.8 | async-start | bytes 3932160 | tf_op jit(solution)/shard_map/reduce_scatter | solution.py:335
  713.6 90.9 %reduce-scatter.7.cloned.1.call-start = ((), (), s32[]{:S(2)}) async-start(), calls=%async_computation.7 | async-start | bytes 3932160 | tf_op jit(solution)/shard_map/reduce_scatter | solution.py:318
  722.2 132.2 %all-gather.10.cloned.1.call-start = ((), (), s32[]{:S(2)}) async-start(), calls=%async_computation.9 | async-start | bytes 3932160 | tf_op jit(solution)/shard_map/all_gather | solution.py:347
  810.3 604.6 %all-reduce.5.cloned.1.call-start = ((), (), s32[]{:S(2)}) async-start(), calls=%async_computation.12 | async-start | bytes 7077888 | tf_op jit(solution)/shard_map/psum | solution.py:451
  986.0 133.5 %copy-start.37 = (bf16[1,2048,48]{2,1,0:T(8,128)(2,1)}, bf16[1,2048,48]{2,1,0:T(8,128)(2,1)S(1)}, u32[]{:S(2)}) copy-start(bf16[1,2048,48]{2,1,0:T(8,128)(2,1)S(1)} %copy.1570) | copy-start | bytes 589828
  1115.3 135.2 %collective-permute-start.6 = (bf16[2,4,512,48]{2,3,1,0:T(8,128)(2,1)}, bf16[2,4,512,48]{2,3,1,0:T(8,128)(2,1)}, u32[]{:S(2)}, u32[]{:S(2)}) collective-permute-start(bf16[2,4,512,48]{2,3,1,0:T(8,128)(2,1)} %select_convert_fusion.2), channel_id=1, source_target_pairs={{0,1},{1,0},{2,3},{3,2},{4,5},{5,4},{6,7},{7,6},{8,9},{9,8},{10,11... | collective-permute-start | bytes 1179656 | tf_op jit(solution)/shard_map/ppermute | solution.py:15
  1161.5 107.7 %collective-permute-start.7 = (bf16[2,4,512,48]{2,3,1,0:T(8,128)(2,1)}, bf16[2,4,512,48]{2,3,1,0:T(8,128)(2,1)}, u32[]{:S(2)}, u32[]{:S(2)}) collective-permute-start(bf16[2,4,512,48]{2,3,1,0:T(8,128)(2,1)} %select_convert_fusion.1), channel_id=1, source_target_pairs={{0,2},{1,3},{2,0},{3,1},{4,6},{5,7},{6,4},{7,5},{8,10},{9,11},{10,... | collective-permute-start | bytes 1179656 | tf_op jit(solution)/shard_map/ppermute | solution.py:15
  1214.2 56.4 %collective-permute-start.9 = (bf16[2,4,512,48]{2,3,1,0:T(8,128)(2,1)}, bf16[2,4,512,48]{2,3,1,0:T(8,128)(2,1)}, u32[]{:S(2)}, u32[]{:S(2)}) collective-permute-start(bf16[2,4,512,48]{2,3,1,0:T(8,128)(2,1)} %select_convert_fusion), channel_id=1, source_target_pairs={{0,4},{1,5},{2,6},{3,7},{4,0},{5,1},{6,2},{7,3},{8,12},{9,13},{10,... | collective-permute-start | bytes 1179656 | tf_op jit(solution)/shard_map/ppermute | solution.py:15
  1270.5 7.2 collective-permute-start.8
  1272.6 23.1 %collective-permute-start.10 = (bf16[2,4,256,48]{2,3,1,0:T(8,128)(2,1)}, bf16[2,4,256,48]{2,3,1,0:T(8,128)(2,1)S(1)}, u32[]{:S(2)}, u32[]{:S(2)}) collective-permute-start(bf16[2,4,256,48]{2,3,1,0:T(8,128)(2,1)} %select_convert_fusion.3), channel_id=1, source_target_pairs={{0,2},{1,3},{2,0},{3,1},{4,6},{5,7},{6,4},{7,5},{8,10},{9,11},{10,... | collective-permute-start | bytes 589832 | tf_op jit(solution)/shard_map/ppermute | solution.py:15
  1295.9 5.3 collective-permute-start.11
  1331.0 131.2 %reduce-scatter.11.cloned.1.call-start = ((), (), s32[]{:S(2)}) async-start(), calls=%async_computation.10 | async-start | bytes 3932160 | tf_op jit(solution)/shard_map/reduce_scatter | solution.py:441
  (383 other events, 2431.6 us)
Sparse Core Ops, SparseCore 0:
  12.9 46.6 all-gather.5
  561.1 42.4 reduce-scatter.4
  607.1 43.9 all-gather.7
  652.8 43.9 all-gather.11
  713.7 43.9 reduce-scatter.8
  760.6 43.9 reduce-scatter.6
  810.4 43.9 all-gather.9
  1331.1 83.7 all-reduce.4
  1418.2 43.9 reduce-scatter.10
where the time goes:
time: 1540 us; the launch traced here: 1520 us
  local copies, waits for them, and re-layouts  527 us (34%)
  matrix products  390 us (25%)
  waiting for transfers between devices  341 us (22%)
  other arithmetic  167 us (11%)
  blocking collectives  56.3 us (4%)
  between operations  21.2 us (1%)
    dot_general x76, matrix products, inner_last(): lax.dot_general(left_side, right_side, (((1,), (1,)), ((), ())), preferre...  170 us
    broadcast_in_dim x239, local copies, waits for them, and re-layouts, undilate(): jnp.where(marks, values[:, None], jnp.asarray(fill_value, values.dtype))  154 us
    dot_general x52, matrix products, matmul(): return jnp.dot(left_side, right_side, preferred_element_type=jnp.float32)  132 us
    dynamic_slice x149, local copies, waits for them, and re-layouts, dilate(): return lax.dynamic_index_in_dim(folded, phase, axis=1, keepdims=False)  126 us
    dot_general x52, matrix products, inner_first(): lax.dot_general(left_side, right_side, (((0,), (0,)), ((), ())), preferre...  87.7 us
    psum x1, waiting for transfers between devices, per_device(): lax.psum(grad_qkv.astype(jnp.bfloat16), 'seq').astype(jnp.float32)  59.3 us
    reduce_sum x24, other arithmetic, attend(): jnp.sum(weights, axis=1)  46.4 us
    reduce_scatter x1, waiting for transfers between devices, per_device(): lax.psum_scatter(matmul(hidden, down_weight).astype(jnp.bfloat16), 'head'...  44 us
  transfers between devices with their start and end apart: 21, of which 10 were waited for; matrix products, arithmetic and copies ran while one was open for 28% of the time, Pallas kernels for 0%

commit v1 on v0

v1 whole, which is shorter than its diff:
```python
import functools
import math

import jax
import jax.numpy as jnp
import numpy as np
from jax import lax
from jax.experimental import pallas as pl
from jax.experimental.pallas import tpu as pltpu
from jax.sharding import PartitionSpec as P

HEAD_WIDTH = 48
SEGMENT_TILES = 1024
LEVELS = 5
RESIDUES = 16
LANES = 128
RING_KEYS = SEGMENT_TILES // 2
ORDER = (0, 8, 4, 12, 2, 6, 10, 14, 1, 3, 5, 7, 9, 11, 13, 15)
SLAB = SEGMENT_TILES // RESIDUES

epsilon = 1e-05
masked_low = -1e30
BF16 = jnp.bfloat16
F32 = jnp.float32
LN2 = math.log(2.0)
SUM_LANE = 2 * HEAD_WIDTH
AUX_LANE = SUM_LANE + 1
AUX_COUNT = 3
VMEM_LIMIT = 52 * 1024 * 1024


def dot(left_side, right_side, left_dim, right_dim):
    return lax.dot_general(
        left_side,
        right_side,
        (((left_dim,), (right_dim,)), ((), ())),
        preferred_element_type=F32,
    )


def class_rows(level):
    low = SEGMENT_TILES >> (level + 1) if level < LEVELS - 1 else 0
    return low, SEGMENT_TILES >> level


def key_class():
    index = np.arange(SEGMENT_TILES)
    found = np.zeros(SEGMENT_TILES, np.int64)
    for level in range(LEVELS):
        found[index < SEGMENT_TILES >> level] = level
    return found


def multiplicity_table():
    classes = key_class()
    table = np.zeros((LEVELS, SEGMENT_TILES + (LEVELS - 1) * RING_KEYS), np.float32)
    for level in range(LEVELS):
        table[level, :SEGMENT_TILES] = 1 + np.minimum(level, classes)
        for ring in range(1, level + 1):
            prefix = SEGMENT_TILES >> ring
            one = np.minimum(level, classes[:prefix]) - ring + 1
            start = SEGMENT_TILES + (ring - 1) * RING_KEYS
            table[level, start : start + RING_KEYS] = np.tile(one, RING_KEYS // prefix)
    return table


def layout(slide_lengths, positions):
    blocks = (slide_lengths + SEGMENT_TILES - 1) // SEGMENT_TILES
    slide_ends = jnp.cumsum(blocks) * SEGMENT_TILES
    slide_starts = slide_ends - blocks * SEGMENT_TILES
    inside = (positions[..., None] >= slide_starts) & (positions[..., None] < slide_ends)
    labels = jnp.arange(slide_lengths.shape[0], dtype=jnp.int32)
    slide_index = jnp.sum(jnp.where(inside, labels, 0), axis=-1)
    offset = positions - jnp.sum(jnp.where(inside, slide_starts, 0), axis=-1)
    length = jnp.sum(jnp.where(inside, slide_lengths, 0), axis=-1)
    return (slide_index, offset < length)


def ring_members(ring, block_count):
    return range((1 << (ring - 1)) // block_count, (1 << ring) // block_count)


def key_bias(slide_lengths, sequence_member, base_head, heads, block_count, row_count):
    local_rings = block_count.bit_length() - 1
    index = np.arange(SEGMENT_TILES)
    order = np.asarray(ORDER)[index // SLAB]
    piece = row_count // RESIDUES
    spot = (index % SLAB) // piece * row_count + index % piece * RESIDUES
    head = base_head + jnp.arange(heads, dtype=jnp.int32)[:, None]
    inner = spot[None, :] + (head + order[None, :]) % RESIDUES
    first_block = sequence_member * block_count
    per_block = []
    for block in range(block_count):
        parts = [(first_block + block) * SEGMENT_TILES + inner]
        for ring in range(1, LEVELS):
            prefix = SEGMENT_TILES >> ring
            if ring <= local_rings:
                start = (block >> (ring - 1) ^ 1) << (ring - 1)
                ids = [first_block + start + t for t in range(1 << (ring - 1))]
            else:
                ids = [
                    (sequence_member ^ x) * block_count + t
                    for x in ring_members(ring, block_count)
                    for t in range(block_count)
                ]
            parts += [one * SEGMENT_TILES + inner[:, :prefix] for one in ids]
        per_block.append(jnp.concatenate(parts, axis=1))
    positions = jnp.stack(per_block, axis=1).astype(jnp.int32)
    slide, valid = layout(slide_lengths, positions)
    own, _ = layout(
        slide_lengths,
        (first_block + jnp.arange(block_count, dtype=jnp.int32)) * SEGMENT_TILES,
    )
    allowed = (slide == own[None, :, None]) & valid
    table = multiplicity_table()
    logs = np.where(table > 0, np.log2(np.maximum(table, 1)), masked_low).astype(np.float32)
    return jnp.where(allowed[:, :, None, :], logs[None, None], masked_low)


def project_kernel(heads, row_count, base_ref, x_ref, w_ref, b_ref, q_ref, kv_ref, held_ref):
    piece = row_count // RESIDUES
    halves = SEGMENT_TILES // row_count
    for half in range(halves):
        x = x_ref[half * row_count : (half + 1) * row_count, :]
        for head in range(heads):
            columns = slice(head * 2 * LANES, (head + 1) * 2 * LANES)
            wide = dot(x, w_ref[:, columns], 1, 0) + b_ref[0:1, columns]
            held_ref[...] = (wide * b_ref[1:2, columns]).astype(BF16)
            for slab in range(RESIDUES):
                residue = lax.rem(base_ref[0] + head + ORDER[slab], RESIDUES)
                source = pl.ds(pl.multiple_of(residue * piece, piece), piece)
                start = slab * SLAB + half * piece
                q_ref[head, 0, start : start + piece, :] = held_ref[source, :LANES]
                kv_ref[head, 0, start : start + piece, :] = held_ref[source, LANES:]


def project(base, rows, weight, bias, heads, row_count):
    total, width = rows.shape
    blocks = total // SEGMENT_TILES
    shape = jax.ShapeDtypeStruct((heads, blocks, SEGMENT_TILES, LANES), BF16)
    spec = pl.BlockSpec((heads, 1, SEGMENT_TILES, LANES), lambda k, *_: (0, k, 0, 0))
    return pl.pallas_call(
        functools.partial(project_kernel, heads, row_count),
        grid_spec=pltpu.PrefetchScalarGridSpec(
            num_scalar_prefetch=1,
            grid=(blocks,),
            in_specs=[
                pl.BlockSpec((SEGMENT_TILES, width), lambda k, *_: (k, 0)),
                pl.BlockSpec(weight.shape, lambda k, *_: (0, 0)),
                pl.BlockSpec(bias.shape, lambda k, *_: (0, 0)),
            ],
            out_specs=[spec, spec],
            scratch_shapes=[pltpu.VMEM((row_count, 2 * LANES), BF16)],
        ),
        out_shape=[shape, shape],
        cost_estimate=pl.CostEstimate(
            flops=2 * total * width * weight.shape[1], bytes_accessed=8 * total * width, transcendentals=0
        ),
        compiler_params=pltpu.CompilerParams(vmem_limit_bytes=VMEM_LIMIT),
        name="project",
    )(base, rows, weight, bias)


def split_three(value):
    high = value.astype(BF16).astype(F32)
    rest = value - high
    middle = rest.astype(BF16).astype(F32)
    return high, middle, rest - middle


def with_aux(rows, value):
    lane = lax.broadcasted_iota(jnp.int32, rows.shape, 1)
    filled = rows.astype(F32)
    for step, part in enumerate(split_three(value)):
        filled = jnp.where(lane == AUX_LANE + step, part, filled)
    return filled.astype(BF16)


def finish(total, peak, q):
    denominator = total[:, SUM_LANE : SUM_LANE + 1]
    lse = peak + jnp.log(denominator) * (1.0 / LN2)
    return total / denominator, with_aux(q, -lse)


def local_pieces(kv_ref, block, ring):
    count = 1 << (ring - 1)
    start = (block // count) ^ 1
    prefix = SEGMENT_TILES >> ring
    return [(start * count + t, prefix) for t in range(count)]


def attend_near_kernel(local_rings, q_ref, kv_ref, bias_ref, o_ref, qa_ref):
    block = pl.program_id(1)
    first = SEGMENT_TILES >> (local_rings + 1)
    for level in range(local_rings + 1):
        low, high = class_rows(level)
        size = min(256, high - low)
        for start in range(low, high, size):
            q = q_ref[0, 0, start : start + size, :]
            keys = [(kv_ref[0, block], 0)]
            place = SEGMENT_TILES
            for ring in range(1, level + 1):
                for other, prefix in local_pieces(kv_ref, block, ring):
                    keys.append((kv_ref[0, other, :prefix], place))
                    place += prefix
            scores = [
                dot(q, kv, 1, 1) + bias_ref[0, 0, level : level + 1, at : at + kv.shape[0]]
                for kv, at in keys
            ]
            peak = functools.reduce(
                jnp.maximum, [jnp.max(s, axis=1, keepdims=True) for s in scores]
            )
            total = sum(
                dot(jnp.exp2(s - peak).astype(BF16), kv, 1, 0) for s, (kv, _) in zip(scores, keys)
            )
            out, extended = finish(total, peak, q)
            o_ref[0, 0, start - first : start - first + size, :] = out
            qa_ref[0, 0, start - first : start - first + size, :] = extended


def attend_near(q, kv, bias):
    heads, blocks = q.shape[:2]
    local_rings = blocks.bit_length() - 1
    rows = SEGMENT_TILES - (SEGMENT_TILES >> (local_rings + 1))
    spec = pl.BlockSpec((1, 1, rows, LANES), lambda h, k: (h, k, 0, 0))
    pairs = heads * blocks * rows * 1400
    return pl.pallas_call(
        functools.partial(attend_near_kernel, local_rings),
        grid=(heads, blocks),
        in_specs=[
            pl.BlockSpec((1, 1, SEGMENT_TILES, LANES), lambda h, k: (h, k, 0, 0)),
            pl.BlockSpec((1, blocks, SEGMENT_TILES, LANES), lambda h, k: (h, 0, 0, 0)),
            pl.BlockSpec((1, 1) + bias.shape[2:], lambda h, k: (h, k, 0, 0)),
        ],
        out_specs=[spec, spec],
        out_shape=[
            jax.ShapeDtypeStruct((heads, blocks, rows, LANES), F32),
            jax.ShapeDtypeStruct((heads, blocks, rows, LANES), BF16),
        ],
        cost_estimate=pl.CostEstimate(
            flops=pairs * 1024, bytes_accessed=heads * blocks * rows * 1500, transcendentals=pairs
        ),
        compiler_params=pltpu.CompilerParams(vmem_limit_bytes=VMEM_LIMIT),
        name="attend_near",
    )(q, kv, bias)


def far_groups(local_rings):
    groups = []
    for level in range(local_rings + 1, LEVELS):
        low, high = class_rows(level)
        groups.append((level, low, high))
    return sorted(groups, key=lambda group: group[1])


def add_bias(scores, bias_ref, block, at, groups, rows):
    width = scores.shape[1]
    parts = []
    for level, low, high in groups:
        if low < rows:
            parts.append(scores[low:high] + bias_ref[0, block, level : level + 1, at : at + width])
    return parts[0] if len(parts) == 1 else jnp.concatenate(parts, axis=0)


def far_score_list(local_rings, blocks, left_ref, kv_ref, far_ref):
    rows = SEGMENT_TILES >> (local_rings + 1)
    pieces = []
    for block in range(blocks):
        pieces.append((0, block, block, SEGMENT_TILES, rows, 0))
    for block in range(blocks):
        place = SEGMENT_TILES
        for ring in range(1, local_rings + 1):
            for other, prefix in local_pieces(kv_ref, block, ring):
                pieces.append((ring, block, other, prefix, rows, place))
                place += prefix
    for ring in range(local_rings + 1, LEVELS):
        pieces.append((ring, None, None, RING_KEYS, SEGMENT_TILES >> ring, SEGMENT_TILES + (ring - 1) * RING_KEYS))
    return pieces


def far_keys(piece, kv_ref, far_ref, local_rings):
    ring, block, other, prefix, rows, place = piece
    if block is not None:
        return kv_ref[0, other, :prefix]
    start = (ring - local_rings - 1) * RING_KEYS
    return far_ref[0, start : start + RING_KEYS, :]


def far_left(piece, left_ref, blocks):
    ring, block, other, prefix, rows, place = piece
    if block is not None:
        return left_ref[0, block, :rows, :]
    return jnp.concatenate([left_ref[0, one, :rows, :] for one in range(blocks)], axis=0)


def pad_rows(value, rows, fill):
    if value.shape[0] == rows:
        return value
    return jnp.concatenate(
        [value, jnp.full((rows - value.shape[0],) + value.shape[1:], fill, value.dtype)], axis=0
    )


def attend_far_kernel(local_rings, blocks, q_ref, kv_ref, far_ref, bias_ref, o_ref, qa_ref):
    rows = SEGMENT_TILES >> (local_rings + 1)
    groups = far_groups(local_rings)
    pieces = far_score_list(local_rings, blocks, q_ref, kv_ref, far_ref)
    held = []
    peaks = [None] * blocks
    for piece in pieces:
        ring, block, other, prefix, count, place = piece
        scores = dot(far_left(piece, q_ref, blocks), far_keys(piece, kv_ref, far_ref, local_rings), 1, 1)
        for one in [block] if block is not None else range(blocks):
            part = scores if block is not None else scores[one * count : (one + 1) * count]
            part = add_bias(part, bias_ref, one, place, groups, count)
            held.append((piece, one, part))
            top = pad_rows(jnp.max(part, axis=1, keepdims=True), rows, masked_low)
            peaks[one] = top if peaks[one] is None else jnp.maximum(peaks[one], top)
    totals = [jnp.zeros((rows, LANES), F32)] * blocks
    for piece in pieces:
        weights = [
            (one, jnp.exp2(part - peaks[one][: piece[4]]).astype(BF16))
            for owner, one, part in held
            if owner is piece
        ]
        joined = weights[0][1] if len(weights) == 1 else jnp.concatenate([w for _, w in weights], axis=0)
        product = dot(joined, far_keys(piece, kv_ref, far_ref, local_rings), 1, 0)
        for at, (one, _) in enumerate(weights):
            part = product[at * piece[4] : (at + 1) * piece[4]]
            totals[one] = totals[one] + pad_rows(part, rows, 0.0)
    for block in range(blocks):
        out, extended = finish(totals[block], peaks[block], q_ref[0, block, :rows, :])
        o_ref[0, block] = out
        qa_ref[0, block] = extended


def attend_far(q, kv, far, bias):
    heads, blocks = q.shape[:2]
    local_rings = blocks.bit_length() - 1
    rows = SEGMENT_TILES >> (local_rings + 1)
    whole = lambda shape: pl.BlockSpec((1,) + shape[1:], lambda h: (h,) + (0,) * (len(shape) - 1))
    shape = (heads, blocks, rows, LANES)
    pairs = heads * blocks * rows * 2600
    return pl.pallas_call(
        functools.partial(attend_far_kernel, local_rings, blocks),
        grid=(heads,),
        in_specs=[
            pl.BlockSpec((1, blocks, rows, LANES), lambda h: (h, 0, 0, 0)),
            whole(kv.shape),
            whole(far.shape),
            whole(bias.shape),
        ],
        out_specs=[whole(shape), whole(shape)],
        out_shape=[jax.ShapeDtypeStruct(shape, F32), jax.ShapeDtypeStruct(shape, BF16)],
        cost_estimate=pl.CostEstimate(
            flops=pairs * 1024, bytes_accessed=heads * 4 * 1024 * 1024, transcendentals=pairs
        ),
        compiler_params=pltpu.CompilerParams(vmem_limit_bytes=VMEM_LIMIT),
        name="attend_far",
    )(q, kv, far, bias)


def placement(heads):
    table = np.zeros((heads * LANES, heads * HEAD_WIDTH), np.float32)
    for head in range(heads):
        for column in range(HEAD_WIDTH):
            table[head * LANES + HEAD_WIDTH + column, head * HEAD_WIDTH + column] = 1
    return table


def pack_kernel(heads, row_count, base_ref, far_ref, near_ref, place_ref, out_ref, held_ref):
    piece = row_count // RESIDUES
    halves = SEGMENT_TILES // row_count
    far_rows = far_ref.shape[2]
    for head in range(heads):
        columns = slice(head * LANES, (head + 1) * LANES)
        for slab in range(RESIDUES):
            residue = lax.rem(base_ref[0] + head + ORDER[slab], RESIDUES)
            for half in range(halves):
                start = slab * SLAB + half * piece
                if start < far_rows:
                    value = far_ref[head, 0, start : start + piece, :]
                else:
                    value = near_ref[head, 0, start - far_rows : start - far_rows + piece, :]
                target = pl.ds(pl.multiple_of(half * row_count + residue * piece, piece), piece)
                held_ref[target, columns] = value.astype(BF16)
    out_ref[...] = dot(held_ref[...], place_ref[...], 1, 0).astype(BF16)


def pack(base, far, near, row_count):
    heads, blocks = far.shape[:2]
    place = jnp.asarray(placement(heads), BF16)
    width = heads * HEAD_WIDTH
    part = lambda shape: pl.BlockSpec((heads, 1) + shape[2:], lambda k, *_: (0, k, 0, 0))
    return pl.pallas_call(
        functools.partial(pack_kernel, heads, row_count),
        grid_spec=pltpu.PrefetchScalarGridSpec(
            num_scalar_prefetch=1,
            grid=(blocks,),
            in_specs=[part(far.shape), part(near.shape), pl.BlockSpec(place.shape, lambda k, *_: (0, 0))],
            out_specs=pl.BlockSpec((SEGMENT_TILES, width), lambda k, *_: (k, 0)),
            scratch_shapes=[pltpu.VMEM((SEGMENT_TILES, heads * LANES), BF16)],
        ),
        out_shape=jax.ShapeDtypeStruct((blocks * SEGMENT_TILES, width), BF16),
        cost_estimate=pl.CostEstimate(
            flops=2 * blocks * SEGMENT_TILES * heads * LANES * width,
            bytes_accessed=blocks * SEGMENT_TILES * heads * LANES * 5,
            transcendentals=0,
        ),
        compiler_params=pltpu.CompilerParams(vmem_limit_bytes=VMEM_LIMIT),
        name="pack",
    )(base, far, near, place)


def unpack_kernel(heads, row_count, base_ref, g_ref, far_ref, near_ref, place_ref, out_ref, held_ref):
    piece = row_count // RESIDUES
    halves = SEGMENT_TILES // row_count
    far_rows = far_ref.shape[2]
    held_ref[...] = dot(g_ref[...], place_ref[...], 1, 1)
    for head in range(heads):
        columns = slice(head * LANES, (head + 1) * LANES)
        for slab in range(RESIDUES):
            residue = lax.rem(base_ref[0] + head + ORDER[slab], RESIDUES)
            for half in range(halves):
                start = slab * SLAB + half * piece
                if start < far_rows:
                    value = far_ref[head, 0, start : start + piece, :]
                else:
                    value = near_ref[head, 0, start - far_rows : start - far_rows + piece, :]
                source = pl.ds(pl.multiple_of(half * row_count + residue * piece, piece), piece)
                grad = held_ref[source, columns]
                delta = jnp.sum(grad * value, axis=1, keepdims=True)
                out_ref[head, 0, start : start + piece, :] = with_aux(grad, -delta)


def unpack(base, grad, far, near, row_count):
    heads, blocks = far.shape[:2]
    place = jnp.asarray(placement(heads), BF16)
    width = heads * HEAD_WIDTH
    part = lambda shape: pl.BlockSpec((heads, 1) + shape[2:], lambda k, *_: (0, k, 0, 0))
    shape = (heads, blocks, SEGMENT_TILES, LANES)
    return pl.pallas_call(
        functools.partial(unpack_kernel, heads, row_count),
        grid_spec=pltpu.PrefetchScalarGridSpec(
            num_scalar_prefetch=1,
            grid=(blocks,),
            in_specs=[
                pl.BlockSpec((SEGMENT_TILES, width), lambda k, *_: (k, 0)),
                part(far.shape),
                part(near.shape),
                pl.BlockSpec(place.shape, lambda k, *_: (0, 0)),
            ],
            out_specs=part(shape),
            scratch_shapes=[pltpu.VMEM((SEGMENT_TILES, heads * LANES), F32)],
        ),
        out_shape=jax.ShapeDtypeStruct(shape, BF16),
        cost_estimate=pl.CostEstimate(
            flops=2 * blocks * SEGMENT_TILES * heads * LANES * width,
            bytes_accessed=blocks * SEGMENT_TILES * heads * LANES * 7,
            transcendentals=0,
        ),
        compiler_params=pltpu.CompilerParams(vmem_limit_bytes=VMEM_LIMIT),
        name="unpack",
    )(base, grad, far, near, place)


def back_near_kernel(local_rings, qa_ref, do_ref, kv_ref, bias_ref, dq_ref, dkv_ref):
    block = pl.program_id(1)
    first = SEGMENT_TILES >> (local_rings + 1)

    @pl.when(block == 0)
    def _():
        dkv_ref[...] = jnp.zeros_like(dkv_ref)

    for level in range(local_rings + 1):
        low, high = class_rows(level)
        size = min(256, high - low)
        for start in range(low, high, size):
            here = slice(start - first, start - first + size)
            q = qa_ref[0, 0, here, :]
            grad = do_ref[0, 0, start : start + size, :]
            q_turned, grad_turned = q.T, grad.T
            keys = [(block, SEGMENT_TILES, 0)]
            place = SEGMENT_TILES
            for ring in range(1, level + 1):
                for other, prefix in local_pieces(kv_ref, block, ring):
                    keys.append((other, prefix, place))
                    place += prefix
            dq = jnp.zeros((size, LANES), F32)
            for other, prefix, at in keys:
                kv = kv_ref[0, other, :prefix]
                scores = dot(q, kv, 1, 1) + bias_ref[0, 0, level : level + 1, at : at + prefix]
                weights = jnp.exp2(scores)
                grads = (weights * dot(grad, kv, 1, 1)).astype(BF16)
                dq = dq + dot(grads, kv, 1, 0)
                dkv_ref[0, other, :, :prefix] += dot(q_turned, grads, 1, 0) + dot(
                    grad_turned, weights.astype(BF16), 1, 0
                )
            dq_ref[0, 0, here, :] = dq


def back_near(qa, do, kv, bias):
    heads, blocks = kv.shape[:2]
    local_rings = blocks.bit_length() - 1
    rows = qa.shape[2]
    spec = pl.BlockSpec((1, 1, rows, LANES), lambda h, k: (h, k, 0, 0))
    pairs = heads * blocks * rows * 1400
    return pl.pallas_call(
        functools.partial(back_near_kernel, local_rings),
        grid=(heads, blocks),
        in_specs=[
            spec,
            pl.BlockSpec((1, 1, SEGMENT_TILES, LANES), lambda h, k: (h, k, 0, 0)),
            pl.BlockSpec((1, blocks, SEGMENT_TILES, LANES), lambda h, k: (h, 0, 0, 0)),
            pl.BlockSpec((1, 1) + bias.shape[2:], lambda h, k: (h, k, 0, 0)),
        ],
        out_specs=[spec, pl.BlockSpec((1, blocks, LANES, SEGMENT_TILES), lambda h, k: (h, 0, 0, 0))],
        out_shape=[
            jax.ShapeDtypeStruct((heads, blocks, rows, LANES), F32),
            jax.ShapeDtypeStruct((heads, blocks, LANES, SEGMENT_TILES), F32),
        ],
        cost_estimate=pl.CostEstimate(
            flops=pairs * 2560, bytes_accessed=heads * blocks * rows * 2500, transcendentals=pairs
        ),
        compiler_params=pltpu.CompilerParams(vmem_limit_bytes=VMEM_LIMIT),
        name="back_near",
    )(qa, do, kv, bias)


def back_far_kernel(
    local_rings, blocks, qa_ref, do_ref, kv_ref, far_ref, bias_ref, dq_ref, dkv_ref, dfar_ref
):
    rows = SEGMENT_TILES >> (local_rings + 1)
    groups = far_groups(local_rings)
    dq_ref[...] = jnp.zeros_like(dq_ref)
    for piece in far_score_list(local_rings, blocks, qa_ref, kv_ref, far_ref):
        ring, block, other, prefix, count, place = piece
        q = far_left(piece, qa_ref, blocks)
        grad = far_left(piece, do_ref, blocks)
        kv = far_keys(piece, kv_ref, far_ref, local_rings)
        raw = dot(q, kv, 1, 1)
        owners = [block] if block is not None else range(blocks)
        parts = [
            add_bias(raw[at * count : (at + 1) * count], bias_ref, one, place, groups, count)
            for at, one in enumerate(owners)
        ]
        scores = parts[0] if len(parts) == 1 else jnp.concatenate(parts, axis=0)
        weights = jnp.exp2(scores)
        grads = (weights * dot(grad, kv, 1, 1)).astype(BF16)
        dq = dot(grads, kv, 1, 0)
        for at, one in enumerate(owners):
            dq_ref[0, one, :count, :] += dq[at * count : (at + 1) * count]
        dkv = dot(q.T, grads, 1, 0) + dot(grad.T, weights.astype(BF16), 1, 0)
        if block is None:
            start = (ring - local_rings - 1) * RING_KEYS
            dfar_ref[0, start : start + RING_KEYS, :] = dkv.T.astype(BF16)
        elif ring == 0:
            dkv_ref[0, other] = dkv
        else:
            dkv_ref[0, other, :, :prefix] += dkv


def back_far(qa, do, kv, far, bias):
    heads, blocks = kv.shape[:2]
    local_rings = blocks.bit_length() - 1
    rows = SEGMENT_TILES >> (local_rings + 1)
    whole = lambda shape: pl.BlockSpec((1,) + shape[1:], lambda h: (h,) + (0,) * (len(shape) - 1))
    pairs = heads * blocks * rows * 2600
    turned = (heads, blocks, LANES, SEGMENT_TILES)
    return pl.pallas_call(
        functools.partial(back_far_kernel, local_rings, blocks),
        grid=(heads,),
        in_specs=[
            whole(qa.shape),
            pl.BlockSpec((1, blocks, rows, LANES), lambda h: (h, 0, 0, 0)),
            whole(kv.shape),
            whole(far.shape),
            whole(bias.shape),
        ],
        out_specs=[whole(qa.shape), whole(turned), whole(far.shape)],
        out_shape=[
            jax.ShapeDtypeStruct(qa.shape, F32),
            jax.ShapeDtypeStruct(turned, F32),
            jax.ShapeDtypeStruct(far.shape, BF16),
        ],
        cost_estimate=pl.CostEstimate(
            flops=pairs * 2560, bytes_accessed=heads * 6 * 1024 * 1024, transcendentals=pairs
        ),
        compiler_params=pltpu.CompilerParams(vmem_limit_bytes=VMEM_LIMIT),
        name="back_far",
    )(qa, do, kv, far, bias)


def collect_kernel(heads, row_count, counts, score_scale, base_ref, *refs):
    dq_far_ref, dq_near_ref, one_ref, two_ref = refs[:4]
    returned = refs[4 : 4 + len(counts)]
    out_ref, held_ref = refs[4 + len(counts) :]
    piece = row_count // RESIDUES
    halves = SEGMENT_TILES // row_count
    far_rows = dq_far_ref.shape[2]
    for head in range(heads):
        held_ref[...] = (one_ref[head, 0] + two_ref[head, 0]).T
        for back_ref, count in zip(returned, counts):
            held_ref[:count, :] += back_ref[head, 0].astype(F32)
        lane = lax.broadcasted_iota(jnp.int32, (piece, LANES), 1)
        factor = jnp.where(lane < HEAD_WIDTH, LN2, jnp.where(lane < SUM_LANE, 1.0, 0.0))
        q_factor = jnp.where(lane < HEAD_WIDTH, score_scale, 0.0)
        for slab in range(RESIDUES):
            residue = lax.rem(base_ref[0] + head + ORDER[slab], RESIDUES)
            for half in range(halves):
                start = slab * SLAB + half * piece
                if start < far_rows:
                    value = dq_far_ref[head, 0, start : start + piece, :]
                else:
                    value = dq_near_ref[head, 0, start - far_rows : start - far_rows + piece, :]
                target = pl.ds(pl.multiple_of(half * row_count + residue * piece, piece), piece)
                at = head * 2 * LANES
                out_ref[target, at : at + LANES] = (value * q_factor).astype(BF16)
                out_ref[target, at + LANES : at + 2 * LANES] = (
                    held_ref[start : start + piece, :] * factor
                ).astype(BF16)


def collect(base, dq_far, dq_near, dkv_one, dkv_two, returned, row_count, score_scale):
    heads, blocks = dq_far.shape[:2]
    counts = tuple(one.shape[2] for one in returned)
    part = lambda shape: pl.BlockSpec((heads, 1) + shape[2:], lambda k, *_: (0, k, 0, 0))
    arrays = (dq_far, dq_near, dkv_one, dkv_two) + tuple(returned)
    width = heads * 2 * LANES
    return pl.pallas_call(
        functools.partial(collect_kernel, heads, row_count, counts, score_scale),
        grid_spec=pltpu.PrefetchScalarGridSpec(
            num_scalar_prefetch=1,
            grid=(blocks,),
            in_specs=[part(one.shape) for one in arrays],
            out_specs=pl.BlockSpec((SEGMENT_TILES, width), lambda k, *_: (k, 0)),
            scratch_shapes=[pltpu.VMEM((SEGMENT_TILES, LANES), F32)],
        ),
        out_shape=jax.ShapeDtypeStruct((blocks * SEGMENT_TILES, width), BF16),
        cost_estimate=pl.CostEstimate(
            flops=blocks * SEGMENT_TILES * width * 8,
            bytes_accessed=blocks * SEGMENT_TILES * width * 10,
            transcendentals=0,
        ),
        compiler_params=pltpu.CompilerParams(vmem_limit_bytes=VMEM_LIMIT),
        name="collect",
    )(base, *arrays)


def residue_major(rows):
    count, width = rows.shape
    return rows.reshape(count // RESIDUES, RESIDUES, width).swapaxes(0, 1).reshape(count, width)


def position_major(rows):
    count, width = rows.shape
    return rows.reshape(RESIDUES, count // RESIDUES, width).swapaxes(0, 1).reshape(count, width)


def norm_forward(values, norm_gain, norm_shift):
    center = values - jnp.mean(values, axis=-1, keepdims=True)
    inverse = lax.rsqrt(jnp.mean(center * center, axis=-1, keepdims=True) + epsilon)
    normed = center * inverse
    return (normed * norm_gain + norm_shift, normed, inverse)


def norm_backward(grad_out, normed, inverse, norm_gain):
    scaled = grad_out * norm_gain
    return inverse * (
        scaled
        - jnp.mean(scaled, axis=-1, keepdims=True)
        - normed * jnp.mean(scaled * normed, axis=-1, keepdims=True)
    )


def gelu_tanh(values):
    return jax.nn.gelu(values, approximate=True)


def from_other(x, axis, flip):
    return lax.ppermute(x, axis, [(i, i ^ flip) for i in range(lax.axis_size(axis))])


def exchange(parts, axis):
    count = lax.axis_size(axis)
    rank = lax.axis_index(axis)
    found = [lax.dynamic_index_in_dim(parts, rank, 0, keepdims=False)]
    for flip in range(1, count):
        sent = lax.dynamic_index_in_dim(parts, rank ^ flip, 0, keepdims=False)
        found.append(from_other(sent, axis, flip))
    return jnp.stack(found)[rank ^ jnp.arange(count)]


def per_device(
    tile_features,
    slide_lengths,
    qkv_weight,
    qv_bias,
    out_weight,
    out_bias,
    attn_gain,
    attn_shift,
    mlp_gain,
    mlp_shift,
    up_weight,
    up_bias,
    down_weight,
    down_bias,
    output_cotangent,
):
    row_count = tile_features.shape[2]
    width = tile_features.shape[3]
    local_width = qkv_weight.shape[2]
    heads = local_width // HEAD_WIDTH
    sequence_member = lax.axis_index("seq")
    head_rank = lax.axis_index("head")
    head_count = lax.axis_size("head")
    extent = row_count * head_count
    blocks = extent // SEGMENT_TILES
    local_rings = blocks.bit_length() - 1
    score_scale = HEAD_WIDTH ** (-0.5)
    query_scale = score_scale / LN2
    base = (head_rank * heads).astype(jnp.int32).reshape(1)

    features = residue_major(tile_features.reshape(row_count, width)).astype(F32)
    normed_one, hat_one, inv_one = norm_forward(features, attn_gain, attn_shift)
    normed_one = normed_one.astype(BF16)
    gathered_one = lax.all_gather(normed_one, "head", axis=0, tiled=True)

    by_head = qkv_weight.reshape(width, 3, heads, HEAD_WIDTH)
    query_weight = jnp.pad(by_head[:, 0], ((0, 0), (0, 0), (0, LANES - HEAD_WIDTH)))
    pair_weight = jnp.pad(
        jnp.concatenate([by_head[:, 1], by_head[:, 2]], axis=-1),
        ((0, 0), (0, 0), (0, LANES - 2 * HEAD_WIDTH)),
    )
    wide = jnp.concatenate([query_weight, pair_weight], axis=-1).reshape(width, heads * 2 * LANES)
    scale_row = np.ones((heads, 2 * LANES), np.float32)
    scale_row[:, :HEAD_WIDTH] = query_scale
    by_head_bias = qv_bias.reshape(2, heads, HEAD_WIDTH)
    ones = np.zeros((heads, LANES - 2 * HEAD_WIDTH), np.float32)
    ones[:, : 1 + AUX_COUNT] = 1.0
    wide_bias = jnp.concatenate(
        [
            by_head_bias[0],
            jnp.zeros((heads, LANES - HEAD_WIDTH), F32),
            jnp.zeros((heads, HEAD_WIDTH), F32),
            by_head_bias[1],
            jnp.asarray(ones),
        ],
        axis=1,
    ).reshape(1, heads * 2 * LANES)
    scale_row = jnp.asarray(scale_row).reshape(1, heads * 2 * LANES)
    bias = key_bias(slide_lengths, sequence_member, head_rank * heads, heads, blocks, row_count)

    q, kv = project(
        base, gathered_one, wide, jnp.concatenate([wide_bias, scale_row], axis=0), heads, row_count
    )
    received = []
    for ring in range(local_rings + 1, LEVELS):
        prefix = SEGMENT_TILES >> ring
        sent = kv[:, :, :prefix].reshape(heads, blocks * prefix, LANES)
        for flip in ring_members(ring, blocks):
            received.append(from_other(sent, "seq", flip))
    up_all = lax.all_gather(up_weight, "head", axis=0)
    down_all = lax.all_gather(down_weight, "head", axis=0)
    out_all = lax.all_gather(out_weight, "head", axis=0, tiled=True)
    up_bias_all = lax.all_gather(up_bias, "head", axis=0)

    o_near, qa_near = attend_near(q, kv, bias)
    far = jnp.concatenate(received, axis=1)
    o_far, qa_far = attend_far(q, kv, far, bias)
    packed = pack(base, o_far, o_near, row_count)
    attn_parts = exchange(packed.reshape(head_count, row_count, local_width), "head")
    attn_low = attn_parts.swapaxes(0, 1).reshape(row_count, width)

    residual = features + dot(attn_low, out_all, 1, 0) + out_bias
    normed_two, hat_two, inv_two = norm_forward(residual, mlp_gain, mlp_shift)
    normed_two = normed_two.astype(BF16)
    cotangent = residue_major(output_cotangent.reshape(row_count, width))
    result = residual + down_bias
    grad_normed_two = 0.0
    grad_up, grad_down, grad_up_bias = [], [], []
    for part in range(head_count):
        pre_act = dot(normed_two, up_all[part], 1, 0) + up_bias_all[part]
        hidden = gelu_tanh(pre_act).astype(BF16)
        result = result + dot(hidden, down_all[part], 1, 0)
        grad_hidden = dot(cotangent, down_all[part], 1, 1)
        grad_down.append(dot(hidden, cotangent, 0, 0).astype(BF16))
        grad_pre = jax.vjp(gelu_tanh, pre_act)[1](grad_hidden)[0].astype(BF16)
        grad_up_bias.append(jnp.sum(grad_pre.astype(F32), axis=0))
        grad_up.append(dot(normed_two, grad_pre, 0, 0).astype(BF16))
        grad_normed_two = grad_normed_two + dot(grad_pre, up_all[part], 1, 1)
    output = position_major(result.astype(BF16)).reshape(tile_features.shape)
    grad_result = cotangent.astype(F32)
    grad_mlp_gain = jnp.sum(grad_normed_two * hat_two, axis=0)
    grad_mlp_shift = jnp.sum(grad_normed_two, axis=0)
    grad_residual = grad_result + norm_backward(grad_normed_two, hat_two, inv_two, mlp_gain)
    grad_down_bias = jnp.sum(grad_result, axis=0)
    grad_out_bias = jnp.sum(grad_residual, axis=0)
    grad_res_low = grad_residual.astype(BF16)
    grad_attn = dot(grad_res_low, out_all, 1, 1).astype(BF16)
    grad_parts = exchange(
        grad_attn.reshape(row_count, head_count, local_width).swapaxes(0, 1), "head"
    ).reshape(extent, local_width)
    grad_out = dot(attn_low, grad_res_low, 0, 0).astype(BF16)

    do = unpack(base, grad_parts, o_far, o_near, row_count)
    dq_far, dkv_far, dfar = back_far(qa_far, do, kv, far, bias)
    returned = []
    at = 0
    for ring in range(local_rings + 1, LEVELS):
        prefix = SEGMENT_TILES >> ring
        for flip in ring_members(ring, blocks):
            sent = dfar[:, at : at + blocks * prefix]
            at += blocks * prefix
            returned.append(
                from_other(sent, "seq", flip).reshape(heads, blocks, prefix, LANES)
            )
    dq_near, dkv_near = back_near(qa_near, do, kv, bias)

    scatter = lambda x: lax.psum_scatter(x, "head", scatter_dimension=0, tiled=False)
    grad_up = lax.psum(scatter(jnp.stack(grad_up)), "seq").astype(F32)
    grad_down = lax.psum(scatter(jnp.stack(grad_down)), "seq").astype(F32)
    grad_out = lax.psum(
        scatter(grad_out.reshape(head_count, local_width, width)), "seq"
    ).astype(F32)
    grad_up_bias = lax.psum(scatter(jnp.stack(grad_up_bias)), "seq")

    grad_proj = collect(base, dq_far, dq_near, dkv_far, dkv_near, returned, row_count, score_scale)
    part_sums = jnp.sum(grad_proj.astype(F32), axis=0).reshape(heads, 2, LANES)
    grad_qv = jnp.stack(
        [
            part_sums[:, 0, :HEAD_WIDTH].reshape(local_width),
            part_sums[:, 1, HEAD_WIDTH : 2 * HEAD_WIDTH].reshape(local_width),
        ]
    )
    grad_wide = dot(gathered_one, grad_proj, 0, 0).reshape(width, heads, 2, LANES)
    grad_qkv = jnp.stack(
        [
            grad_wide[:, :, 0, :HEAD_WIDTH].reshape(width, local_width),
            grad_wide[:, :, 1, :HEAD_WIDTH].reshape(width, local_width),
            grad_wide[:, :, 1, HEAD_WIDTH : 2 * HEAD_WIDTH].reshape(width, local_width),
        ],
        axis=1,
    )
    grad_normed_one = lax.psum_scatter(
        dot(grad_proj, wide, 1, 1).astype(BF16), "head", scatter_dimension=0, tiled=True
    ).astype(F32)
    grad_attn_gain = jnp.sum(grad_normed_one * hat_one, axis=0)
    grad_attn_shift = jnp.sum(grad_normed_one, axis=0)
    grad_features = grad_residual + norm_backward(grad_normed_one, hat_one, inv_one, attn_gain)
    grad_qkv = lax.psum(grad_qkv.astype(BF16), "seq").astype(F32)
    grad_qv = lax.psum(grad_qv, "seq")
    norm_totals = lax.psum(
        (
            grad_attn_gain,
            grad_attn_shift,
            grad_mlp_gain,
            grad_mlp_shift,
            grad_out_bias,
            grad_down_bias,
        ),
        ("head", "seq"),
    )
    return (
        output,
        position_major(grad_features).reshape(tile_features.shape),
        grad_qkv,
        grad_qv,
        grad_out,
        norm_totals[4],
        norm_totals[0],
        norm_totals[1],
        norm_totals[2],
        norm_totals[3],
        grad_up,
        grad_up_bias,
        grad_down,
        norm_totals[5],
    )


def solution(mesh):
    in_specs = (
        P("seq", "head", None, None),
        P(),
        P(None, None, "head"),
        P(None, "head"),
        P("head", None),
        P(),
        P(),
        P(),
        P(),
        P(),
        P(None, "head"),
        P("head"),
        P("head", None),
        P(),
        P("seq", "head", None, None),
    )
    out_specs = (
        P("seq", "head", None, None),
        P("seq", "head", None, None),
        P(None, None, "head"),
        P(None, "head"),
        P("head", None),
        P(),
        P(),
        P(),
        P(),
        P(),
        P(None, "head"),
        P("head"),
        P("head", None),
        P(),
    )
    return jax.shard_map(
        per_device, mesh=mesh, in_specs=in_specs, out_specs=out_specs, check_vma=False
    )
```

time: 1540 us -> 544 us (0.35); the launches traced: 1520 us -> 537 us
  local copies, waits for them, and re-layouts: 527 us -> 50 us
  matrix products: 390 us -> 67.3 us
  waiting for transfers between devices: 341 us -> 179 us
  other arithmetic: 167 us -> 30.3 us
  Pallas kernels: 0 us -> 87.4 us
  blocking collectives: 56.3 us -> 81.7 us
  starting transfers between devices: 10.4 us -> 26.1 us
    dot_general x180 -> x29, matrix products: 390 us -> 67.3 us  [dot(): lax.dot_general(left_side, right_side, (((left_dim,), (right_dim,)), ((),...]
    dynamic_slice x281 -> x5, local copies, waits for them, and re-layouts: 180 us -> 1.87 us  [the longest x3 1.72 us: exchange(): sent = lax.dynamic_index_in_dim(parts, rank ^ flip, 0, keepdims=False)]
    reduce_scatter x4 -> x1, waiting for transfers between devices: 163 us -> 6.13 us  [per_device(): lax.psum_scatter(dot(grad_proj, wide, 1, 1).astype(BF16), 'head', scatter...]
    broadcast_in_dim x240 -> x2, local copies, waits for them, and re-layouts: 154 us -> 0.01 us  [the longest x1 0.01 us: per_device(): jnp.zeros((heads, LANES - HEAD_WIDTH), F32)]
    pallas_call x0 -> x8, Pallas kernels: none -> 87.4 us  [the longest x1 20.4 us: back_near(): pl.pallas_call(functools.partial(back_near_kernel, local_rings), grid=(he...]
    another operation x77 -> x8, local copies, waits for them, and re-layouts: 55.7 us -> 2.44 us  [the longest x32 18.5 us: dilate(): source.reshape((source.shape[0] // dilation_step, dilation_step) + source...]
    reduce_sum x32 -> x4, other arithmetic: 55.8 us -> 3.7 us  [the longest x1 3.03 us: per_device(): part_sums = jnp.sum(grad_proj.astype(F32), axis=0).reshape(heads, 2, LANES)]
    all_gather x3, waiting for transfers between devices: 93.8 us -> 55.8 us  [the longest x1 47.5 us: per_device(): down_all = lax.all_gather(down_weight, 'head', axis=0)]
  transfers between devices with their start and end apart: 21 -> 29, of which waited for: 10 -> 14; matrix products, arithmetic and copies ran while one was open for 28% -> 21% of each run, Pallas kernels for 0% -> 16%
where the time goes in v1:
time: 544 us; the launch traced here: 537 us
  waiting for transfers between devices  179 us (33%)
  Pallas kernels  87.4 us (16%)
  blocking collectives  81.7 us (15%)
  matrix products  67.3 us (12%)
  local copies, waits for them, and re-layouts  50 us (9%)
  other arithmetic  30.3 us (6%)
  starting transfers between devices  26.1 us (5%)
  between operations  15.2 us (3%)
    dot_general x29, matrix products, dot(): lax.dot_general(left_side, right_side, (((left_dim,), (right_dim,)), ((),...  67.3 us
    all_gather x1, waiting for transfers between devices, per_device(): down_all = lax.all_gather(down_weight, 'head', axis=0)  47.5 us
    psum x1, waiting for transfers between devices, per_device(): grad_qkv = lax.psum(grad_qkv.astype(BF16), 'seq').astype(F32)  43.4 us
    psum x1, blocking collectives, per_device(): lax.psum((grad_attn_gain, grad_attn_shift, grad_mlp_gain, grad_mlp_shift,...  41.5 us
    ppermute x20, waiting for transfers between devices, from_other(): lax.ppermute(x, axis, [(i, i ^ flip) for i in range(lax.axis_size(axis))])  38.6 us
    all_gather x1, waiting for transfers between devices, per_device(): gathered_one = lax.all_gather(normed_one, 'head', axis=0, tiled=True)  26.8 us
    ppermute x20, starting transfers between devices, from_other(): lax.ppermute(x, axis, [(i, i ^ flip) for i in range(lax.axis_size(axis))])  25.4 us
    pallas_call x1, Pallas kernels, back_near(): pl.pallas_call(functools.partial(back_near_kernel, local_rings), grid=(he...  20.4 us
  transfers between devices with their start and end apart: 29, of which 14 were waited for; matrix products, arithmetic and copies ran while one was open for 21% of the time, Pallas kernels for 16%

profile of v1, /device:TPU:0, one launch (start us, length us, event | category | flops | bytes accessed | tf_op | source)
XLA Modules:
  0.0 536.7 jit_solution(18265016091311739391)
XLA Ops:
  21.8 10.0 %all-gather.3 = f32[4,1,768]{2,1,0:T(1,128)S(1)} all-gather(f32[1,1,768]{2,1,0:T(1,128)S(1)} %reshape.343), channel_id=3, replica_groups=mesh['head'=4,'seq'=8] {'head'}, dimensions={0}, use_global_device_ids=true | all-gather | bytes 15360 | tf_op jit(solution)/shard_map/all_gather | solution.py:767
  32.5 26.8 %all-gather.9.cloned.1.call-done.x_ref = bf16[2048,768]{1,0:T(8,128)(2,1)} async-done(((bf16[512,768]{1,0:T(8,128)(2,1)}), bf16[2048,768]{1,0:T(8,128)(2,1)}) %all-gather.9.cloned.1.call-update) | async-done | bytes 3145744 | tf_op jit(solution)/shard_map/all_gather | solution.py:728
  59.3 7.2 %project.1 = (bf16[4,2,1024,128]{3,2,1,0:T(8,128)(2,1)}, bf16[4,2,1024,128]{3,2,1,0:T(8,128)(2,1)}) custom-call(s32[1]{0:T(128)} %bitcast.3.base_ref, bf16[2048,768]{1,0:T(8,128)(2,1)} %all-gather.9.cloned.1.call-done.x_ref, bf16[768,1024]{1,0:T(8,128)(2,1)S(1)} %bitcast.152, f32[2,1024]{1,0:T(2,128)S(1)} %pad_maximum_fusion.6.b_ref), custom_call_target="tpu_custom_call" | custom-call | flops 3221225472 | bytes 12582912 | tf_op jit(solution)/shard_map/project/pallas_call | solution.py:142
  74.1 17.0 %attend_near.1 = (f32[4,2,768,128]{3,2,1,0:T(8,128)}, bf16[4,2,768,128]{3,2,1,0:T(8,128)(2,1)}) custom-call(bf16[4,2,1024,128]{3,2,1,0:T(8,128)(2,1)} %get-tuple-element.25.q_ref, bf16[4,2,1024,128]{3,2,1,0:T(8,128)(2,1)} %get-tuple-element.26.kv_ref, f32[4,2,5,3072]{3,2,1,0:T(8,128)S(1)} %broadcast_select_fusion.bias_ref), custom_call_target="tpu_custom_call" | custom-call | flops 8808038400 | bytes 9216000 | tf_op jit(solution)/shard_map/attend_near/pallas_call | solution.py:227
  102.9 10.7 %attend_far.1 = (f32[4,2,256,128]{3,2,1,0:T(8,128)}, bf16[4,2,256,128]{3,2,1,0:T(8,128)(2,1)S(1)}) custom-call(bf16[4,2,1024,128]{3,2,1,0:T(8,128)(2,1)} %get-tuple-element.25.q_ref, bf16[4,2,1024,128]{3,2,1,0:T(8,128)(2,1)} %get-tuple-element.26.kv_ref, bf16[4,1536,128]{2,1,0:T(8,128)(2,1)} %copy-done.29, f32[4,2,5,3072]{3,2,1,0:T(8,128)S(1)} %broadcast_select_fusion.bias_ref), custom_call_target="tpu_custom_call" | custom-call | flops 5452595200 | bytes 16777216 | tf_op jit(solution)/shard_map/attend_far/pallas_call | solution.py:344
  123.8 6.6 %collective-permute-done.9 = bf16[512,192]{0,1:T(8,128)(2,1)S(1)} collective-permute-done((bf16[512,192]{0,1:T(8,128)(2,1)}, bf16[512,192]{0,1:T(8,128)(2,1)S(1)}, u32[]{:S(2)}, u32[]{:S(2)}) %collective-permute-start.9) | collective-permute-done | bytes 196640 | tf_op jit(solution)/shard_map/ppermute | solution.py:681
  130.3 4.1 collective-permute-done.8
  134.4 4.4 collective-permute-done.7
  147.6 8.3 %all-gather.13.cloned.1.call-done = bf16[3072,768]{1,0:T(8,128)(2,1)} async-done(((bf16[768,768]{1,0:T(8,128)(2,1)}), bf16[3072,768]{1,0:T(8,128)(2,1)}) %all-gather.13.cloned.1.call-update) | async-done | bytes 4718608 | tf_op jit(solution)/shard_map/all_gather | solution.py:764
  166.7 47.5 %all-gather.15.cloned.1.call-done = bf16[3072,768]{1,0:T(8,128)(2,1)} async-done(((bf16[768,768]{1,0:T(8,128)(2,1)}), bf16[3072,768]{1,0:T(8,128)(2,1)}) %all-gather.15.cloned.1.call-update) | async-done | bytes 4718608 | tf_op jit(solution)/shard_map/all_gather | solution.py:765
  258.8 6.6 %collective-permute-done.12 = bf16[512,192]{0,1:T(8,128)(2,1)S(1)} collective-permute-done((bf16[512,192]{0,1:T(8,128)(2,1)S(1)}, bf16[512,192]{0,1:T(8,128)(2,1)S(1)}, u32[]{:S(2)}, u32[]{:S(2)}) %collective-permute-start.12) | collective-permute-done | bytes 196640 | tf_op jit(solution)/shard_map/ppermute | solution.py:681
  271.4 5.3 unpack.1.do_ref
  276.8 15.0 %back_far.1 = (f32[4,2,256,128]{3,2,1,0:T(8,128)}, f32[4,2,128,1024]{3,2,1,0:T(8,128)}, bf16[4,1536,128]{2,1,0:T(8,128)(2,1)}) custom-call(bf16[4,2,256,128]{3,2,1,0:T(8,128)(2,1)S(1)} %get-tuple-element.29.qa_ref, bf16[4,2,1024,128]{3,2,1,0:T(8,128)(2,1)} %unpack.1.do_ref, bf16[4,2,1024,128]{3,2,1,0:T(8,128)(2,1)} %get-tuple-element.26.kv_ref, ...), custom_call_target="tpu_custom_call" | custom-call | flops 13631488000 | bytes 25165824 | tf_op jit(solution)/shard_map/back_far/pallas_call | solution.py:570
  299.8 7.4 %collective-permute-done.16 = bf16[4,128,128]{2,1,0:T(8,128)(2,1)S(1)} collective-permute-done((bf16[4,128,128]{2,1,0:T(8,128)(2,1)S(1)}, bf16[4,128,128]{2,1,0:T(8,128)(2,1)S(1)}, u32[]{:S(2)}, u32[]{:S(2)}) %collective-permute-start.16) | collective-permute-done | bytes 131104 | tf_op jit(solution)/shard_map/ppermute | solution.py:681
  312.5 20.4 %back_near.1 = (f32[4,2,768,128]{3,2,1,0:T(8,128)}, f32[4,2,128,1024]{3,2,1,0:T(8,128)}) custom-call(bf16[4,2,768,128]{3,2,1,0:T(8,128)(2,1)} %get-tuple-element.31.qa_ref, bf16[4,2,1024,128]{3,2,1,0:T(8,128)(2,1)} %unpack.1.do_ref, bf16[4,2,1024,128]{3,2,1,0:T(8,128)(2,1)} %get-tuple-element.26.kv_ref, f32[4,2,5,3072]{3,2,1,0:T(8,128)S(1)} %copy-done.2), custom_call_target="tpu_custom_call" | custom-call | flops 22020096000 | bytes 15360000 | tf_op jit(solution)/shard_map/back_near/pallas_call | solution.py:508
  332.9 8.4 %collect.1 = bf16[2048,1024]{1,0:T(8,128)(2,1)} custom-call(s32[1]{0:T(128)} %bitcast.3.base_ref, f32[4,2,256,128]{3,2,1,0:T(8,128)} %get-tuple-element.30.refs_0_, f32[4,2,768,128]{3,2,1,0:T(8,128)} %get-tuple-element.32.refs_1_, f32[4,2,128,1024]{3,2,1,0:T(8,128)} %get-tuple-element.33.refs_2_, f32[4,2,128,1024]{3,2,1,0:T(8,128)} %get-tuple-element.34.refs_3_, ...), custom_call_target="tpu_custom_call" | custom-call | flops 16777216 | bytes 20971520 | tf_op jit(solution)/shard_map/collect/pallas_call | solution.py:630
  341.3 7.7 %convolution_convert_fusion = bf16[2048,768]{1,0:T(8,128)(2,1)} fusion(bf16[2048,1024]{1,0:T(8,128)(2,1)} %collect.1, bf16[768,1024]{1,0:T(8,128)(2,1)S(1)} %bitcast.153), kind=kOutput, calls=%fused_computation.5 | convolution fusion | flops 3222798336 | bytes 8912896 | tf_op jit(solution)/shard_map/dot_general | solution.py:33
  366.3 5.6 %fusion.95 = (bf16[768,4,1,48]{3,2,1,0:T(2,128)(2,1)S(1)}, bf16[768,4,1,48]{3,2,1,0:T(2,128)(2,1)}, bf16[768,4,1,48]{3,2,1,0:T(2,128)(2,1)}) fusion(bf16[768,4,2,128]{3,2,1,0:T(2,128)(2,1)S(1)} %reshape.297), kind=kLoop, calls=%fused_computation.223 | loop fusion | bytes 1769472 | tf_op jit(solution)/shard_map/slice | solution.py:840
  380.3 5.9 %reduce-scatter.17.cloned.1.call-done = bf16[1,768,768]{2,1,0:T(8,128)(2,1)} async-done(((bf16[4,768,768]{2,1,0:T(8,128)(2,1)}), bf16[1,768,768]{2,1,0:T(8,128)(2,1)}) %reduce-scatter.17.cloned.1.call-update) | async-done | bytes 1179664
  393.3 15.5 %all-reduce.4 = f32[4,768]{1,0:T(4,128)S(1)} all-reduce(f32[4,768]{1,0:T(4,128)S(1)} %pad_maximum_fusion.5), channel_id=8, replica_groups=mesh['head'=4,'seq'=8] {'head'}, use_global_device_ids=true, to_apply=%region_35.36.clone | all-reduce | flops 3072 | bytes 24576
  412.8 14.7 %all-reduce.7 = (f32[2,192]{1,0:T(2,128)}, f32[768]{0:T(1024)}) all-reduce(f32[2,192]{1,0:T(2,128)S(1)} %pad_maximum_fusion.7, f32[768]{0:T(1024)S(1)} %dynamic-slice_reduce_fusion), channel_id=1, replica_groups=mesh['head'=4,'seq'=8] {'seq'}, use_global_device_ids=true, to_apply=%region_16.17 | all-reduce | flops 1152 | bytes 9216 | tf_op jit(solution)/shard_map/psum | solution.py:853
  427.6 6.1 %reduce-scatter.11.cloned.1.call-done = bf16[512,768]{1,0:T(8,128)(2,1)} async-done(((bf16[2048,768]{1,0:T(8,128)(2,1)}), bf16[512,768]{1,0:T(8,128)(2,1)}) %reduce-scatter.11.cloned.1.call-update) | async-done | bytes 786448 | tf_op jit(solution)/shard_map/reduce_scatter | solution.py:846
  438.4 41.5 %all-reduce.6 = (f32[768]{0:T(1024)}, f32[768]{0:T(1024)}, f32[768]{0:T(1024)}, f32[768]{0:T(1024)}, f32[768]{0:T(1024)}, /*index=5*/f32[768]{0:T(1024)}) all-reduce(f32[768]{0:T(1024)S(1)} %get-tuple-element.67, f32[768]{0:T(1024)S(1)} %get-tuple-element.38, ...), channel_id=1, replica_groups=mesh['head'=4,'seq'=8] {'head','seq'}, use_global_device_ids=true, to_apply=%region_20.21 | all-reduce | flops 4608 | bytes 36864 | tf_op jit(solution)/shard_map/psum | solution.py:854
  479.9 43.4 %all-reduce.11.cloned.1.call-done = (bf16[768,3,192]{0,2,1:T(8,128)(2,1)}, bf16[192,768]{1,0:T(8,128)(2,1)}, bf16[768,768]{1,0:T(8,128)(2,1)}, bf16[768,768]{1,0:T(8,128)(2,1)}) async-done(((bf16[768,3,192]{0,2,1:T(8,128)(2,1)}, bf16[192,768]{1,0:T(8,128)(2,1)}, bf16[768,768]{1,0:T(8,128)(2,1)}, bf16[768,768]{1,0:T(8,128)(2,1)}), (bf16[768,3,192]{0,2,1:T(8,128)(2,1)}, bf16[192,768]{1,0:T(8,128)(2,1)}, ...) | async-done | bytes 3538960 | tf_op jit(solution)/shard_map/psum | solution.py:852
  (339 shorter events, 175.4 us)
Async XLA Ops:
  7.2 52.1 %all-gather.9.cloned.1.call-start = ((), (), s32[]{:S(2)}) async-start(), calls=%async_computation.4 | async-start | bytes 3932160 | tf_op jit(solution)/shard_map/all_gather | solution.py:728
  12.2 130.3 %all-gather.11.cloned.1.call-start = ((), (), s32[]{:S(2)}) async-start(), calls=%async_computation.5 | async-start | bytes 1474560 | tf_op jit(solution)/shard_map/all_gather | solution.py:766
  13.0 142.9 %all-gather.13.cloned.1.call-start = ((), (), s32[]{:S(2)}) async-start(), calls=%async_computation.7 | async-start | bytes 5898240 | tf_op jit(solution)/shard_map/all_gather | solution.py:764
  13.7 200.5 %all-gather.15.cloned.1.call-start = ((), (), s32[]{:S(2)}) async-start(), calls=%async_computation.8 | async-start | bytes 5898240 | tf_op jit(solution)/shard_map/all_gather | solution.py:765
  14.3 366.0 %reduce-scatter.13.cloned.1.call-start = ((), (), s32[]{:S(2)}) async-start(), calls=%async_computation.9 | async-start | bytes 1474560
  68.5 25.9 %collective-permute-start.1 = (bf16[4,256,128]{2,1,0:T(8,128)(2,1)S(1)}, bf16[4,256,128]{2,1,0:T(8,128)(2,1)S(1)}, u32[]{:S(2)}, u32[]{:S(2)}) collective-permute-start(bf16[4,256,128]{2,1,0:T(8,128)(2,1)S(1)} %bitcast.199), channel_id=1, source_target_pairs={{0,2},{1,3},{2,0},{3,1},{4,6},{5,7},{6,4},{7,5},{8,10},{9,11},{10,... | collective-permute-start | bytes 786440 | tf_op jit(solution)/shard_map/ppermute | solution.py:681
  70.1 24.8 %collective-permute-start.2 = (bf16[4,256,128]{2,1,0:T(8,128)(2,1)S(1)}, bf16[4,256,128]{2,1,0:T(8,128)(2,1)S(1)}, u32[]{:S(2)}, u32[]{:S(2)}) collective-permute-start(bf16[4,256,128]{2,1,0:T(8,128)(2,1)S(1)} %bitcast.200), channel_id=1, source_target_pairs={{0,3},{1,2},{2,1},{3,0},{4,7},{5,6},{6,5},{7,4},{8,11},{9,10},{10,... | collective-permute-start | bytes 786440 | tf_op jit(solution)/shard_map/ppermute | solution.py:681
  71.0 23.9 %collective-permute-start.3 = (bf16[4,128,128]{2,1,0:T(8,128)(2,1)S(1)}, bf16[4,128,128]{2,1,0:T(8,128)(2,1)S(1)}, u32[]{:S(2)}, u32[]{:S(2)}) collective-permute-start(bf16[4,128,128]{2,1,0:T(8,128)(2,1)S(1)} %bitcast.209), channel_id=1, source_target_pairs={{0,4},{1,5},{2,6},{3,7},{4,0},{5,1},{6,2},{7,3},{8,12},{9,13},{10,... | collective-permute-start | bytes 393224 | tf_op jit(solution)/shard_map/ppermute | solution.py:681
  73.5 21.5 %collective-permute-start.4 = (bf16[4,128,128]{2,1,0:T(8,128)(2,1)S(1)}, bf16[4,128,128]{2,1,0:T(8,128)(2,1)S(1)}, u32[]{:S(2)}, u32[]{:S(2)}) collective-permute-start(bf16[4,128,128]{2,1,0:T(8,128)(2,1)S(1)} %bitcast.210), channel_id=1, source_target_pairs={{0,5},{1,4},{2,7},{3,6},{4,1},{5,0},{6,3},{7,2},{8,13},{9,12},{10,... | collective-permute-start | bytes 393224 | tf_op jit(solution)/shard_map/ppermute | solution.py:681
  74.0 17.1 %collective-permute-start = (bf16[4,512,128]{2,1,0:T(8,128)(2,1)S(1)}, bf16[4,512,128]{2,1,0:T(8,128)(2,1)S(1)}, u32[]{:S(2)}, u32[]{:S(2)}) collective-permute-start(bf16[4,512,128]{2,1,0:T(8,128)(2,1)S(1)} %bitcast.191), channel_id=1, source_target_pairs={{0,1},{1,0},{2,3},{3,2},{4,5},{5,4},{6,7},{7,6},{8,9},{9,8},{10,11... | collective-permute-start | bytes 1572872 | tf_op jit(solution)/shard_map/ppermute | solution.py:681
  117.9 12.5 %collective-permute-start.9 = (bf16[512,192]{0,1:T(8,128)(2,1)}, bf16[512,192]{0,1:T(8,128)(2,1)S(1)}, u32[]{:S(2)}, u32[]{:S(2)}) collective-permute-start(bf16[512,192]{0,1:T(8,128)(2,1)} %bitcast.203), channel_id=1, source_target_pairs={{0,24},{8,16},{16,8},{24,0},{1,25},{9,17},{17,9},{25,1},{2,26},{10... | collective-permute-start | bytes 589832 | tf_op jit(solution)/shard_map/ppermute | solution.py:681
  119.6 14.8 %collective-permute-start.8 = (bf16[512,192]{0,1:T(8,128)(2,1)S(1)}, bf16[512,192]{0,1:T(8,128)(2,1)S(1)}, u32[]{:S(2)}, u32[]{:S(2)}) collective-permute-start(bf16[512,192]{0,1:T(8,128)(2,1)S(1)} %bitcast.204), channel_id=1, source_target_pairs={{0,16},{8,24},{16,0},{24,8},{1,17},{9,25},{17,1},{25,9},{2,18},{10... | collective-permute-start | bytes 589832 | tf_op jit(solution)/shard_map/ppermute | solution.py:681
  121.9 16.9 %collective-permute-start.7 = (bf16[512,192]{0,1:T(8,128)(2,1)}, bf16[512,192]{0,1:T(8,128)(2,1)}, u32[]{:S(2)}, u32[]{:S(2)}) collective-permute-start(bf16[512,192]{0,1:T(8,128)(2,1)} %bitcast.205), channel_id=1, source_target_pairs={{0,8},{8,0},{16,24},{24,16},{1,9},{9,1},{17,25},{25,17},{2,10},{10... | collective-permute-start | bytes 589832 | tf_op jit(solution)/shard_map/ppermute | solution.py:681
  232.2 148.1 %reduce-scatter.15.cloned.1.call-start = ((), (), s32[]{:S(2)}) async-start(), calls=%async_computation.10 | async-start | bytes 5898240
  240.2 146.1 %reduce-scatter.17.cloned.1.call-start = ((), (), s32[]{:S(2)}) async-start(), calls=%async_computation.11 | async-start | bytes 5898240
  250.2 183.5 %reduce-scatter.11.cloned.1.call-start = ((), (), s32[]{:S(2)}) async-start(), calls=%async_computation.6 | async-start | bytes 3932160 | tf_op jit(solution)/shard_map/reduce_scatter | solution.py:846
  292.9 40.0 %collective-permute-start.13 = (bf16[4,512,128]{2,1,0:T(8,128)(2,1)S(1)}, bf16[4,512,128]{2,1,0:T(8,128)(2,1)S(1)}, u32[]{:S(2)}, u32[]{:S(2)}) collective-permute-start(bf16[4,512,128]{2,1,0:T(8,128)(2,1)S(1)} %slice.171), channel_id=1, source_target_pairs={{0,1},{1,0},{2,3},{3,2},{4,5},{5,4},{6,7},{7,6},{8,9},{9,8},{10,11... | collective-permute-start | bytes 1572872 | tf_op jit(solution)/shard_map/ppermute | solution.py:681
  294.1 13.0 %collective-permute-start.16 = (bf16[4,128,128]{2,1,0:T(8,128)(2,1)S(1)}, bf16[4,128,128]{2,1,0:T(8,128)(2,1)S(1)}, u32[]{:S(2)}, u32[]{:S(2)}) collective-permute-start(bf16[4,128,128]{2,1,0:T(8,128)(2,1)S(1)} %get-tuple-element.75), channel_id=1, source_target_pairs={{0,4},{1,5},{2,6},{3,7},{4,0},{5,1},{6,2},{7,3},{8,12},{9,13},{10,... | collective-permute-start | bytes 393224 | tf_op jit(solution)/shard_map/ppermute | solution.py:681
  296.6 13.4 %collective-permute-start.17 = (bf16[4,128,128]{2,1,0:T(8,128)(2,1)S(1)}, bf16[4,128,128]{2,1,0:T(8,128)(2,1)S(1)}, u32[]{:S(2)}, u32[]{:S(2)}) collective-permute-start(bf16[4,128,128]{2,1,0:T(8,128)(2,1)S(1)} %get-tuple-element.74), channel_id=1, source_target_pairs={{0,5},{1,4},{2,7},{3,6},{4,1},{5,0},{6,3},{7,2},{8,13},{9,12},{10,... | collective-permute-start | bytes 393224 | tf_op jit(solution)/shard_map/ppermute | solution.py:681
  298.0 34.9 %collective-permute-start.14 = (bf16[4,256,128]{2,1,0:T(8,128)(2,1)S(1)}, bf16[4,256,128]{2,1,0:T(8,128)(2,1)S(1)}, u32[]{:S(2)}, u32[]{:S(2)}) collective-permute-start(bf16[4,256,128]{2,1,0:T(8,128)(2,1)S(1)} %get-tuple-element.77), channel_id=1, source_target_pairs={{0,2},{1,3},{2,0},{3,1},{4,6},{5,7},{6,4},{7,5},{8,10},{9,11},{10,... | collective-permute-start | bytes 786440 | tf_op jit(solution)/shard_map/ppermute | solution.py:681
  299.6 33.3 %collective-permute-start.15 = (bf16[4,256,128]{2,1,0:T(8,128)(2,1)S(1)}, bf16[4,256,128]{2,1,0:T(8,128)(2,1)S(1)}, u32[]{:S(2)}, u32[]{:S(2)}) collective-permute-start(bf16[4,256,128]{2,1,0:T(8,128)(2,1)S(1)} %get-tuple-element.76), channel_id=1, source_target_pairs={{0,3},{1,2},{2,1},{3,0},{4,7},{5,6},{6,5},{7,4},{8,11},{9,10},{10,... | collective-permute-start | bytes 786440 | tf_op jit(solution)/shard_map/ppermute | solution.py:681
  307.1 25.8 %collective-permute-start.18 = (bf16[4,128,128]{2,1,0:T(8,128)(2,1)S(1)}, bf16[4,128,128]{2,1,0:T(8,128)(2,1)S(1)}, u32[]{:S(2)}, u32[]{:S(2)}) collective-permute-start(bf16[4,128,128]{2,1,0:T(8,128)(2,1)S(1)} %get-tuple-element.73), channel_id=1, source_target_pairs={{0,6},{1,7},{2,4},{3,5},{4,2},{5,3},{6,0},{7,1},{8,14},{9,15},{10,... | collective-permute-start | bytes 393224 | tf_op jit(solution)/shard_map/ppermute | solution.py:681
  310.1 22.8 %collective-permute-start.19 = (bf16[4,128,128]{2,1,0:T(8,128)(2,1)S(1)}, bf16[4,128,128]{2,1,0:T(8,128)(2,1)S(1)}, u32[]{:S(2)}, u32[]{:S(2)}) collective-permute-start(bf16[4,128,128]{2,1,0:T(8,128)(2,1)S(1)} %get-tuple-element.72), channel_id=1, source_target_pairs={{0,7},{1,6},{2,5},{3,4},{4,3},{5,2},{6,1},{7,0},{8,15},{9,14},{10,... | collective-permute-start | bytes 393224 | tf_op jit(solution)/shard_map/ppermute | solution.py:681
  349.0 174.2 %all-reduce.11.cloned.1.call-start = ((), (), s32[]{:S(2)}) async-start(), calls=%async_computation.12 | async-start | bytes 7077888 | tf_op jit(solution)/shard_map/psum | solution.py:852
  (77 other events, 440.2 us)
Sparse Core Ops, SparseCore 0:
  12.3 46.8 all-gather.8
  61.1 27.7 all-gather.10
  90.7 65.1 all-gather.12
  157.6 56.6 all-gather.14
  232.3 33.4 reduce-scatter.12
  268.7 57.4 reduce-scatter.14
  329.1 57.0 reduce-scatter.16
  389.2 44.4 reduce-scatter.10
  436.9 86.2 all-reduce.10
